TPU v7x, 256 devices: a whole 4x4x8 slice. The times are simulated.
256 devices in a mesh: inst: 64 (over z_lo, y, x), tp: 4 (over z_hi, core).
Axes of the slice: x: 4, y: 4, z: 8 (z_hi: 2, z_lo: 4; z = z_hi * 4 + z_lo), core: 2. Of those that a mesh axis runs over, the one named last changes fastest.
Arguments:
- pool_kv: bfloat16 [3072, 2, 8, 64, 128], P('inst', None, 'tp'), may hold values from -6 to 6
- block_table: int32 [256, 24], P('inst'), may hold values from 0 to 47
- context_len: int32 [64, 4], replicated, may hold values from 1 to 1536, 3840 in all within a row
- partner: int32 [64], replicated, may hold values from 0 to 63, as said below
- mig_slot: int32 [64], replicated, may hold values from 0 to 3
- prompt_kv: bfloat16 [3072, 2, 8, 64, 128], P(('inst', 'tp')), may hold values from -6 to 6
- prompt_dest: int32 [3072, 1], replicated, may hold values from 0 to 63; in each aligned block of 48 rows (0 to 47, 48 to 95, ...) at most 2 rows name the same one
- queries: bfloat16 [320, 4, 64, 128], P('inst', None, 'tp'), may hold values from -15 to 15
- step_kv: bfloat16 [320, 4, 2, 8, 128], P('inst', None, None, 'tp'), may hold values from -6 to 6
Outputs:
- attn_out: bfloat16 [320, 4, 64, 128], P('inst', None, 'tp')
Inputs may be any that keep to these rules, and one draw needn't show every extreme that they name: partner[partner[i]] = i; partner[i] differs from i in exactly one of the three lowest bits. `context_len`: each instance's 4 lengths sum to 3840. `prompt_dest`: among the 48 prompt pages held by one instance, no instance is named more than 2 times.
All inputs are finite; a program needn't handle non-finite values.
Results may differ from a plain program's by a relative error of at most 0.0066.
Values may be sent and summed in bfloat16 or wider, within the bound.
A program may use at most 128 MiB of HBM per device.

v0:
```python
import math

import jax
import jax.numpy as jnp
from jax import lax
from jax.sharding import PartitionSpec as P

CAP = 2


def swapped(value, axis, apart):
    mask = 2**apart
    pairs = [(source, source ^ mask) for source in range(lax.axis_size(axis))]
    return lax.ppermute(value, axis, pairs)


def rope_freqs(size):
    half = size // 2
    ratio = jnp.arange(half, dtype=jnp.float32) * (2.0 / size)
    base = jnp.exp(-ratio * math.log(500000.0))
    wavelength = 2.0 * math.pi / base
    smooth = (8192.0 / wavelength - 1.0) / 3.0
    blended = (1.0 - smooth) * base / 8.0 + smooth * base
    return jnp.where(wavelength < 2048.0, base, jnp.where(wavelength > 8192.0, base / 8.0, blended))


def rotate(vector, position):
    half = vector.shape[-1] // 2
    angles = position.astype(jnp.float32)[..., None] * rope_freqs(vector.shape[-1])
    cosine = jnp.cos(angles)
    sine = jnp.sin(angles)
    first = vector[..., :half]
    second = vector[..., half:]
    return jnp.concatenate(
        [first * cosine - second * sine, second * cosine + first * sine], axis=-1
    )


def group_heads(tensor, kv_heads):
    steps, heads, width = tensor.shape
    return (
        tensor.reshape(steps, kv_heads, heads // kv_heads, width)
        .transpose(1, 0, 2, 3)
        .reshape(kv_heads, -1, width)
    )


def ungroup_heads(tensor, steps):
    kv_heads, rows, width = tensor.shape
    return (
        tensor.reshape(kv_heads, steps, rows // steps, width)
        .transpose(1, 0, 2, 3)
        .reshape(steps, -1, width)
    )


def rotate_query(query, length, kv_heads):
    positions = length + jnp.arange(query.shape[0], dtype=jnp.int32)
    turned = rotate(query.astype(jnp.float32), positions[:, None]).astype(jnp.bfloat16)
    return group_heads(turned, kv_heads)


def page_stats(qrot, keys, values, valid):
    scores = jnp.einsum(
        "hrd,phtd->hrpt", qrot, keys, preferred_element_type=jnp.float32
    ) / math.sqrt(qrot.shape[-1])
    masked = jnp.where(valid, scores, -1e30)
    top = jnp.max(masked, axis=3)
    weights = jnp.where(valid, jnp.exp(masked - top[..., None]), 0.0).astype(jnp.bfloat16)
    total = jnp.sum(weights.astype(jnp.float32), axis=3)
    acc = jnp.einsum("hrpt,phtd->hrpd", weights, values, preferred_element_type=jnp.float32)
    return (top, total, acc)


def fold_pages(stats):
    top, total, acc = stats
    best = jnp.max(top, axis=2)
    scale = jnp.exp(top - best[..., None])
    return (best, jnp.sum(scale * total, axis=2), jnp.sum(scale[..., None] * acc, axis=2))


def join_parts(first, second):
    best = jnp.maximum(first[0], second[0])
    left = jnp.exp(first[0] - best)
    right = jnp.exp(second[0] - best)
    return (
        best,
        left * first[1] + right * second[1],
        left[..., None] * first[2] + right[..., None] * second[2],
    )


def new_page_stats(qrot, kv_steps, length):
    steps = kv_steps.shape[0]
    positions = length + jnp.arange(steps, dtype=jnp.int32)
    keys = rotate(kv_steps[:, 0].astype(jnp.float32), positions[:, None]).astype(jnp.bfloat16)
    keys = keys.transpose(1, 0, 2)[None]
    values = kv_steps[:, 1].transpose(1, 0, 2)[None]
    rows = qrot.shape[1]
    row_step = jnp.arange(rows, dtype=jnp.int32) // (rows // steps)
    valid = jnp.arange(steps, dtype=jnp.int32)[None, None, :] <= row_step[:, None, None]
    return fold_pages(page_stats(qrot, keys, values, valid))


def per_device(
    pool_kv, block_table, context_len, partner, mig_slot, prompt_kv, prompt_dest, queries, step_kv
):
    inst_count = lax.axis_size("inst")
    here = lax.axis_index("inst")
    kv_heads = step_kv.shape[3]
    slots = block_table.shape[0]
    page_len = pool_kv.shape[3]
    max_pages = block_table.shape[1]
    steps = queries.shape[1]
    my_slot = mig_slot[here]
    mate = partner[here]
    mate_len = context_len[mate, mig_slot[mate]]
    own_len = context_len[here]
    slot_ids = jnp.arange(slots, dtype=jnp.int32)
    post_len = jnp.where(slot_ids == my_slot, mate_len, own_len)
    rotate_all = jax.vmap(lambda query, length: rotate_query(query, length, kv_heads))
    res_q = rotate_all(queries[:slots], post_len)
    positions = (
        jnp.arange(max_pages, dtype=jnp.int32)[:, None] * page_len
        + jnp.arange(page_len, dtype=jnp.int32)[None, :]
    )

    def cache_part(qrot, pages, length):
        return fold_pages(page_stats(qrot, pages[:, 0], pages[:, 1], positions < length))

    leaving = pool_kv[block_table[my_slot]]
    arrived = jnp.zeros_like(leaving)
    for bit in range(3):
        got = swapped(leaving, "inst", bit)
        arrived = jnp.where(jnp.bitwise_xor(here, 1 << bit) == mate, got, arrived)
    pages = pool_kv[block_table]
    pages = jnp.where((slot_ids == my_slot)[:, None, None, None, None, None], arrived[None], pages)
    cache = jax.vmap(cache_part)(res_q, pages, post_len)
    fresh = jax.vmap(new_page_stats)(res_q, step_kv[:slots], post_len)
    merged = jax.vmap(join_parts)(cache, fresh)
    res_out = jax.vmap(lambda part: ungroup_heads(part[2] / part[1][..., None], steps))(merged)
    mine_pages = lax.all_to_all(prompt_kv, "tp", split_axis=2, concat_axis=0, tiled=True)
    rows_here = mine_pages.shape[0]
    dest_grid = prompt_dest[:, 0].reshape(inst_count, rows_here)
    my_dests = dest_grid[here]
    counts = jnp.sum((dest_grid == here).astype(jnp.int32), axis=1)
    new_len = jnp.sum(counts) * page_len
    new_q = rotate_query(queries[slots], new_len, kv_heads)
    row_ids = jnp.arange(rows_here, dtype=jnp.int32)
    same = (my_dests[:, None] == my_dests[None, :]) & (row_ids[None, :] < row_ids[:, None])
    rank = jnp.sum(same.astype(jnp.int32), axis=1)
    target = my_dests * CAP + rank
    slot_grid = jnp.arange(inst_count * CAP, dtype=jnp.int32)
    match = slot_grid[:, None] == target[None, :]
    source = jnp.sum(jnp.where(match, row_ids[None, :], 0), axis=1)
    filled = jnp.any(match, axis=1)
    outbox = jnp.where(
        filled[:, None, None, None, None], mine_pages[source], jnp.zeros((), jnp.bfloat16)
    )
    outbox = outbox.reshape((inst_count, CAP) + mine_pages.shape[1:])
    inbox = lax.all_to_all(outbox, "inst", split_axis=0, concat_axis=0, tiled=True)
    inbox = inbox.reshape((inst_count * CAP,) + mine_pages.shape[1:])
    live = (jnp.arange(CAP, dtype=jnp.int32)[None, :] < counts[:, None]).reshape(-1)
    valid = jnp.broadcast_to(live[:, None], (inst_count * CAP, page_len))
    prompt_part = fold_pages(page_stats(new_q, inbox[:, 0], inbox[:, 1], valid))
    new_fresh = new_page_stats(new_q, step_kv[slots], new_len)
    new_best, new_sum, new_acc = join_parts(prompt_part, new_fresh)
    new_out = ungroup_heads(new_acc / new_sum[..., None], steps)
    return jnp.concatenate([res_out, new_out[None]], axis=0).astype(jnp.bfloat16)


def solution(mesh):
    placed = (
        P("inst", None, "tp", None, None),
        P("inst", None),
        P(),
        P(),
        P(),
        P(("inst", "tp"), None, None, None, None),
        P(),
        P("inst", None, "tp", None),
        P("inst", None, None, "tp", None),
    )
    return jax.shard_map(
        per_device,
        mesh=mesh,
        in_specs=placed,
        out_specs=P("inst", None, "tp", None),
        check_vma=False,
    )
```

profile of v0, /device:TPU:2, one launch (start us, length us, event | category | flops | bytes accessed | tf_op | source)
XLA Modules:
  0.0 354.0 jit_solution(9652761423963092686)
XLA Ops:
  0.0 4.7 %copy.82 = bf16[12,2,8,64,128]{4,3,1,0,2:T(8,128)(2,1)} copy(bf16[12,2,8,64,128]{4,3,2,1,0:T(8,128)(2,1)} %param.14) | data formatting | bytes 6291456 | tf_op args[5]
  4.8 8.6 %all-to-all-start = ((bf16[12,2,8,64,128]{4,3,1,0,2:T(8,128)(2,1)}), bf16[12,2,8,64,128]{4,3,1,0,2:T(8,128)(2,1)}, u32[]{:S(2)}, u32[]{:S(2)}) async-start(bf16[12,2,8,64,128]{4,3,1,0,2:T(8,128)(2,1)} %copy.82), calls=%async_computation | async-start | bytes 6291456 | tf_op jit(solution)/shard_map/all_to_all | solution.py:142
  13.3 0.5 broadcast.416
  13.9 1.3 fusion.43
  15.2 0.2 convert_reduce_fusion.3
  15.5 0.2 broadcast_in_dim.177
  15.8 57.0 %all-to-all-done = bf16[12,2,8,64,128]{4,3,1,0,2:T(8,128)(2,1)} async-done(((bf16[12,2,8,64,128]{4,3,1,0,2:T(8,128)(2,1)}), bf16[12,2,8,64,128]{4,3,1,0,2:T(8,128)(2,1)}, u32[]{:S(2)}, u32[]{:S(2)}) %all-to-all-start) | async-done | bytes 3145760 | tf_op jit(solution)/shard_map/all_to_all | solution.py:142
  72.8 4.6 %copy.84 = bf16[4,12,2,2,64,128]{5,4,3,2,1,0:T(8,128)(2,1)} copy(bf16[4,12,2,2,64,128]{5,4,2,1,3,0:T(8,128)(2,1)} %bitcast.42) | data formatting | bytes 6291456 | tf_op jit(solution)/shard_map/all_to_all | solution.py:142
  77.4 8.3 %gather_fusion.2 = bf16[128,2,2,64,128]{4,3,2,1,0:T(8,128)(2,1)} fusion(bf16[48,2,2,64,128]{4,3,2,1,0:T(8,128)(2,1)} %bitcast.232, s32[1024]{0:T(1024)S(1)} %pad_clamp_fusion), kind=kCustom, calls=%fused_computation.2 | custom fusion | bytes 16777728 | tf_op jit(solution)/shard_map/gather | solution.py:158
  85.7 17.4 %broadcast_select_fusion = bf16[64,2,2,2,64,128]{5,1,4,3,2,0:T(2,128)(2,1)} fusion(pred[64,2]{1,0:T(8,128)(4,1)S(1)} %broadcast_in_dim.177, bf16[64,2,2,2,64,128]{5,4,3,2,1,0:T(8,128)(2,1)} %bitcast.233), kind=kLoop, calls=%fused_computation.3 | loop fusion | flops 4194304 | bytes 16777344 | tf_op jit(solution)/shard_map/jit(_where)/select_n | solution.py:157
  103.1 24.4 %all-to-all-start.1 = ((bf16[64,2,2,2,64,128]{5,1,4,3,2,0:T(2,128)(2,1)}), bf16[64,2,2,2,64,128]{5,1,4,3,2,0:T(2,128)(2,1)}, u32[]{:S(2)}, u32[]{:S(2)}) async-start(bf16[64,2,2,2,64,128]{5,1,4,3,2,0:T(2,128)(2,1)} %broadcast_select_fusion), calls=%async_computation.1 | async-start | bytes 16777216 | tf_op jit(solution)/shard_map/all_to_all | solution.py:161
  127.5 0.6 dynamic_slice.22
  130.0 0.7 fusion.65
  132.6 1.9 gather_fusion
  134.5 1.5 collective-permute-start
  136.0 2.1 collective-permute-start.1
  138.0 1.5 collective-permute-start.2
  142.9 6.0 %gather_fusion.1 = bf16[96,2,2,64,128]{4,3,2,1,0:T(8,128)(2,1)} fusion(bf16[48,2,2,64,128]{4,3,2,1,0:T(8,128)(2,1)S(1)} %copy-done, s32[1024]{0:T(1024)S(1)} %pad_clamp_fusion.1), kind=kCustom, calls=%fused_computation.1 | custom fusion | bytes 12583296 | tf_op jit(solution)/shard_map/gather | solution.py:136
  148.9 0.2 dynamic-slice_reduce_fusion
  149.8 0.7 dynamic_slice.24
  150.5 1.3 broadcast_select_fusion.1
  151.9 0.1 multiply_cosine_fusion
  152.0 0.6 fusion.64
  152.9 0.2 fusion.67
  153.2 0.5 copy-done.6
  154.7 0.7 lt.121
  155.7 0.2 fusion.66
  156.1 0.5 copy-done.13
  156.7 0.6 iota_compare_fusion.4
  157.3 0.6 subtract_exponential_fusion.3
  157.9 0.6 subtract_exponential_fusion.2
  158.7 78.4 %collective-permute-done = bf16[24,2,2,64,128]{4,3,2,1,0:T(8,128)(2,1)} collective-permute-done((bf16[24,2,2,64,128]{4,3,2,1,0:T(8,128)(2,1)}, bf16[24,2,2,64,128]{4,3,2,1,0:T(8,128)(2,1)}, u32[]{:S(2)}, u32[]{:S(2)}) %collective-permute-start) | collective-permute-done | bytes 1572896 | tf_op jit(solution)/shard_map/ppermute | solution.py:14
  237.1 14.0 %collective-permute-done.1 = bf16[24,2,2,64,128]{4,3,2,1,0:T(8,128)(2,1)} collective-permute-done((bf16[24,2,2,64,128]{4,3,2,1,0:T(8,128)(2,1)}, bf16[24,2,2,64,128]{4,3,2,1,0:T(8,128)(2,1)}, u32[]{:S(2)}, u32[]{:S(2)}) %collective-permute-start.1) | collective-permute-done | bytes 1572896 | tf_op jit(solution)/shard_map/ppermute | solution.py:14
  251.0 54.3 %collective-permute-done.2 = bf16[24,2,2,64,128]{4,3,2,1,0:T(8,128)(2,1)} collective-permute-done((bf16[24,2,2,64,128]{4,3,2,1,0:T(8,128)(2,1)}, bf16[24,2,2,64,128]{4,3,2,1,0:T(8,128)(2,1)}, u32[]{:S(2)}, u32[]{:S(2)}) %collective-permute-start.2) | collective-permute-done | bytes 1572896 | tf_op jit(solution)/shard_map/ppermute | solution.py:14
  305.4 9.0 %copy_select_fusion = bf16[4,24,2,2,64,128]{5,4,1,3,0,2:T(8,128)(2,1)} fusion(bf16[4,24,2,2,64,128]{5,4,3,2,1,0:T(8,128)(2,1)} %bitcast.234, pred[4]{0:T(512)(128)(4,1)S(1)} %iota_compare_fusion.4, bf16[24,2,2,64,128]{4,3,2,1,0:T(8,128)(2,1)} %collective-permute-done, bf16[24,2,2,64,128]{4,3,2,1,0:T(8,128)(2,1)} %collective-permute-done.1, ...), kind=kLoop, calls=%fused_computation.4 | loop fusion | flops 5505024 | bytes 17301512 | tf_op jit(solution)/shard_map/jit(_where)/select_n | solution.py:137
  314.4 5.1 %fusion.7 = (f32[4,2,32,24]{2,3,1,0:T(8,128)S(1)}, f32[4,2,32,24,64]{4,2,3,1,0:T(8,128)S(1)}) fusion(pred[4,24,64]{2,1,0:T(8,128)(4,1)S(1)} %broadcast_compare_fusion, bf16[4,24,2,2,64,128]{5,4,1,3,0,2:T(8,128)(2,1)} %copy_select_fusion, bf16[4,4,2,8,64]{4,3,2,1,0:T(8,128)(2,1)S(1)} %get-tuple-element.24, bf16[4,4,2,8,64]{4,3,2,1,0:T(8,128)(2,1)S(1)} %get-tuple-element.23), kind=kOutput, calls=%fused_computation.21 | convolution fusion | flops 101967872 | bytes 4814848 | tf_op jit(solution)/shard_map/vmap(hrd,phtd->hrpt)/dot_general | solution.py:64
  319.5 2.1 convert_reduce_fusion
  321.9 3.3 fusion.6
  325.2 0.3 fusion.17
  325.5 9.3 %copy.86 = bf16[64,2,2,2,64,128]{5,1,0,4,3,2:T(2,128)(2,1)S(1)} copy(bf16[64,2,2,2,64,128]{5,1,4,3,2,0:T(2,128)(2,1)} %all-to-all-done.1) | data formatting | bytes 16777216 | tf_op jit(solution)/shard_map/all_to_all | solution.py:161
  334.9 2.4 slice_bitcast_fusion
  337.3 1.7 fusion.59
  339.1 0.4 convert_reduce_fusion.1
  339.5 0.2 multiply_reduce_fusion.1
  339.8 4.5 %copy.90 = bf16[2,32,128,64]{3,1,2,0:T(8,128)(2,1)} copy(bf16[2,32,128,64]{2,1,3,0:T(8,128)(2,1)S(1)} %get-tuple-element.22) | data formatting | bytes 2097152 | tf_op jit(solution)/shard_map/convert_element_type | solution.py:69
  344.4 8.7 %fusion.1 = f32[2,32,128]{2,1,0:T(8,128)S(1)} fusion(f32[2,32,128]{1,2,0:T(8,128)S(1)} %copy.88, bf16[2,32,128,64]{3,1,2,0:T(8,128)(2,1)} %copy.90, bf16[128,2,64,128]{3,0,2,1:T(8,128)(2,1)} %slice_bitcast_fusion), kind=kOutput, calls=%fused_computation.9 | convolution fusion | flops 136306688 | bytes 5308416 | tf_op jit(solution)/shard_map/hrpt,phtd->hrpd/dot_general | solution.py:71
  353.1 0.2 fusion.24
  353.3 0.6 pad_maximum_fusion
  (95 shorter events, 2.4 us)
Async XLA Ops:
  0.0 132.5 %copy-start = (bf16[48,2,2,64,128]{4,3,2,1,0:T(8,128)(2,1)S(1)}, bf16[48,2,2,64,128]{4,3,2,1,0:T(8,128)(2,1)}, u32[]{:S(2)}) copy-start(bf16[48,2,2,64,128]{4,3,2,1,0:T(8,128)(2,1)} %param.9) | copy-start | bytes 9437188
  4.8 9.1 %copy-start.8 = (s32[3072,1]{0,1:T(1,128)S(1)}, s32[3072,1]{0,1:T(1,128)}, u32[]{:S(2)}) copy-start(s32[3072,1]{0,1:T(1,128)} %param.15) | copy-start | bytes 36868
  4.8 68.1 %all-to-all-start = ((bf16[12,2,8,64,128]{4,3,1,0,2:T(8,128)(2,1)}), bf16[12,2,8,64,128]{4,3,1,0,2:T(8,128)(2,1)}, u32[]{:S(2)}, u32[]{:S(2)}) async-start(bf16[12,2,8,64,128]{4,3,1,0,2:T(8,128)(2,1)} %copy.82), calls=%async_computation | async-start | bytes 6291456 | tf_op jit(solution)/shard_map/all_to_all | solution.py:142
  103.1 24.5 %copy-start.22 = (s32[64]{0:T(128)S(1)}, s32[64]{0:T(128)}, u32[]{:S(2)}) copy-start(s32[64]{0:T(128)} %param.12) | copy-start | bytes 772
  103.1 26.9 %copy-start.16 = (s32[64]{0:T(128)S(1)}, s32[64]{0:T(128)}, u32[]{:S(2)}) copy-start(s32[64]{0:T(128)} %param.13) | copy-start | bytes 772
  103.1 29.4 %copy-start.17 = (s32[4,24]{1,0:T(4,128)S(1)}, s32[4,24]{1,0:T(4,128)}, u32[]{:S(2)}) copy-start(s32[4,24]{1,0:T(4,128)} %param.10) | copy-start | bytes 1156
  103.1 222.4 %all-to-all-start.1 = ((bf16[64,2,2,2,64,128]{5,1,4,3,2,0:T(2,128)(2,1)}), bf16[64,2,2,2,64,128]{5,1,4,3,2,0:T(2,128)(2,1)}, u32[]{:S(2)}, u32[]{:S(2)}) async-start(bf16[64,2,2,2,64,128]{5,1,4,3,2,0:T(2,128)(2,1)} %broadcast_select_fusion), calls=%async_computation.1 | async-start | bytes 16777216 | tf_op jit(solution)/shard_map/all_to_all | solution.py:161
  134.5 102.6 %collective-permute-start = (bf16[24,2,2,64,128]{4,3,2,1,0:T(8,128)(2,1)}, bf16[24,2,2,64,128]{4,3,2,1,0:T(8,128)(2,1)}, u32[]{:S(2)}, u32[]{:S(2)}) collective-permute-start(bf16[24,2,2,64,128]{4,3,2,1,0:T(8,128)(2,1)} %gather_fusion), channel_id=1, source_target_pairs={{0,16},{4,20},{8,24},{12,28},{16,0},{20,4},{24,8},{28,12},{32,48},... | collective-permute-start | bytes 4718600 | tf_op jit(solution)/shard_map/ppermute | solution.py:14
  136.0 115.1 %collective-permute-start.1 = (bf16[24,2,2,64,128]{4,3,2,1,0:T(8,128)(2,1)}, bf16[24,2,2,64,128]{4,3,2,1,0:T(8,128)(2,1)}, u32[]{:S(2)}, u32[]{:S(2)}) collective-permute-start(bf16[24,2,2,64,128]{4,3,2,1,0:T(8,128)(2,1)} %gather_fusion), channel_id=1, source_target_pairs={{0,8},{4,12},{8,0},{12,4},{16,24},{20,28},{24,16},{28,20},{32,40},... | collective-permute-start | bytes 4718600 | tf_op jit(solution)/shard_map/ppermute | solution.py:14
  138.0 167.3 %collective-permute-start.2 = (bf16[24,2,2,64,128]{4,3,2,1,0:T(8,128)(2,1)}, bf16[24,2,2,64,128]{4,3,2,1,0:T(8,128)(2,1)}, u32[]{:S(2)}, u32[]{:S(2)}) collective-permute-start(bf16[24,2,2,64,128]{4,3,2,1,0:T(8,128)(2,1)} %gather_fusion), channel_id=1, source_target_pairs={{0,4},{4,0},{8,12},{12,8},{16,20},{20,16},{24,28},{28,24},{32,36},... | collective-permute-start | bytes 4718600 | tf_op jit(solution)/shard_map/ppermute | solution.py:14
  142.8 6.0 %copy-start.15 = (s32[64,4]{0,1:T(4,128)S(1)}, s32[64,4]{0,1:T(4,128)}, u32[]{:S(2)}) copy-start(s32[64,4]{0,1:T(4,128)} %param.11) | copy-start | bytes 3076
  142.8 9.2 %copy-start.3 = (bf16[5,4,2,2,128]{4,3,2,1,0:T(2,128)(2,1)S(1)}, bf16[5,4,2,2,128]{4,3,2,1,0:T(2,128)(2,1)}, u32[]{:S(2)}) copy-start(bf16[5,4,2,2,128]{4,3,2,1,0:T(2,128)(2,1)} %param.17) | copy-start | bytes 61444
  142.8 9.9 %copy-start.2 = (bf16[5,4,16,128]{3,2,1,0:T(8,128)(2,1)S(1)}, bf16[5,4,16,128]{3,2,1,0:T(8,128)(2,1)}, u32[]{:S(2)}) copy-start(bf16[5,4,16,128]{3,2,1,0:T(8,128)(2,1)} %param.16) | copy-start | bytes 245764
  142.9 12.6 %slice-start = ((bf16[5,4,2,2,128]{4,3,2,1,0:T(2,128)(2,1)}), bf16[1,4,2,2,128]{4,3,2,1,0:T(2,128)(2,1)S(1)}, s32[]{:S(2)}) async-start(bf16[5,4,2,2,128]{4,3,2,1,0:T(2,128)(2,1)} %param.17), calls=%async_computation.2 | async-start | bytes 8192 | tf_op jit(solution)/shard_map/slice | solution.py:166
  150.5 154.9 %copy-start.18 = (pred[32,4]{0,1:T(4,128)(4,1)}, pred[32,4]{0,1:T(4,128)(4,1)S(1)}, u32[]{:S(2)}) copy-start(pred[32,4]{0,1:T(4,128)(4,1)S(1)} %iota_compare_fusion.3) | copy-start | bytes 388
  153.1 0.6 copy-start.6
  155.7 158.7 %copy-start.4 = (bf16[4,2,8,64]{3,2,1,0:T(8,128)(2,1)}, bf16[4,2,8,64]{3,2,1,0:T(8,128)(2,1)S(1)}, u32[]{:S(2)}) copy-start(bf16[4,2,8,64]{3,2,1,0:T(8,128)(2,1)S(1)} %get-tuple-element.26) | copy-start | bytes 24580
  156.0 0.6 copy-start.13
  156.0 158.4 %copy-start.9 = (f32[2,32]{1,0:T(2,128)}, f32[2,32]{1,0:T(2,128)S(1)}, u32[]{:S(2)}) copy-start(f32[2,32]{1,0:T(2,128)S(1)} %get-tuple-element.40) | copy-start | bytes 772
  321.8 3.3 copy-start.7
  321.8 3.3 copy-start.11
  321.8 3.3 copy-start.12
  321.8 3.3 copy-start.19
  334.9 2.5 copy-start.5
  334.9 2.4 copy-start.20
  344.3 9.7 %copy-start.1 = (bf16[48,2,2,64,128]{4,3,2,1,0:T(8,128)(2,1)S(1)}, bf16[48,2,2,64,128]{4,3,2,1,0:T(8,128)(2,1)}, u32[]{:S(2)}) copy-start(bf16[48,2,2,64,128]{4,3,2,1,0:T(8,128)(2,1)} %param.9) | copy-start | bytes 9437188
  344.4 8.7 %copy-start.10 = (f32[2,32]{1,0:T(2,128)S(1)}, f32[2,32]{1,0:T(2,128)}, u32[]{:S(2)}) copy-start(f32[2,32]{1,0:T(2,128)} %copy-done.9) | copy-start | bytes 772
  344.4 8.7 %copy-start.14 = (f32[2,32,4]{1,2,0:T(4,128)S(1)}, f32[2,32,4]{1,2,0:T(4,128)}, u32[]{:S(2)}) copy-start(f32[2,32,4]{1,2,0:T(4,128)} %copy-done.13) | copy-start | bytes 3076
  344.4 8.7 %copy-start.21 = (f32[2,32]{1,0:T(2,128)S(1)}, f32[2,32]{1,0:T(2,128)}, u32[]{:S(2)}) copy-start(f32[2,32]{1,0:T(2,128)} %subtract_exponential_fusion.3) | copy-start | bytes 772
where the time goes:
time: 360 us; the launch traced here: 354 us
  waiting for transfers between devices  204 us (57%)
  local copies, waits for them, and re-layouts  48 us (13%)
  starting transfers between devices  38 us (11%)
  other arithmetic  35.8 us (10%)
  matrix products  19.7 us (5%)
  between operations  8.8 us (2%)
    ppermute x3, waiting for transfers between devices, swapped(): return lax.ppermute(value, axis, pairs)  147 us
    all_to_all x1, waiting for transfers between devices, per_device(): lax.all_to_all(prompt_kv, 'tp', split_axis=2, concat_axis=0, tiled=True)  57 us
    all_to_all x1, starting transfers between devices, per_device(): lax.all_to_all(outbox, 'inst', split_axis=0, concat_axis=0, tiled=True)  24.4 us
    select_n x1, other arithmetic, per_device(): jnp.where(filled[:, None, None, None, None], mine_pages[source], jnp.zero...  17.4 us
    dot_general x4, matrix products, page_stats(): jnp.einsum('hrpt,phtd->hrpd', weights, values, preferred_element_type=jnp...  12.4 us
    all_to_all x1, local copies, waits for them, and re-layouts, per_device(): lax.all_to_all(outbox, 'inst', split_axis=0, concat_axis=0, tiled=True)  9.33 us
    select_n x1, other arithmetic, per_device(): jnp.where((slot_ids == my_slot)[:, None, None, None, None, None], arrived...  9.02 us
    all_to_all x1, starting transfers between devices, per_device(): lax.all_to_all(prompt_kv, 'tp', split_axis=2, concat_axis=0, tiled=True)  8.59 us
  transfers between devices with their start and end apart: 5, of which 4 were waited for; matrix products, arithmetic and copies ran while one was open for 11% of the time, Pallas kernels for 0%

commit v1 on v0

v1 whole, which is shorter than its diff:
```python
import math

import jax
import jax.numpy as jnp
from jax import lax
from jax.experimental import pallas as pl
from jax.experimental.pallas import tpu as pltpu
from jax.sharding import PartitionSpec as P

MESH = pl.DeviceIdType.MESH
NEG = -1e30
F32 = jnp.float32
BF16 = jnp.bfloat16
HD = 128
SCALE = 1.0 / math.sqrt(HD)


def rope_freqs(size):
    half = size // 2
    ratio = jnp.arange(half, dtype=jnp.float32) * (2.0 / size)
    base = jnp.exp(-ratio * math.log(500000.0))
    wavelength = 2.0 * math.pi / base
    smooth = (8192.0 / wavelength - 1.0) / 3.0
    blended = (1.0 - smooth) * base / 8.0 + smooth * base
    return jnp.where(wavelength < 2048.0, base, jnp.where(wavelength > 8192.0, base / 8.0, blended))


def rotate(vector, cosine, sine):
    half = vector.shape[-1] // 2
    first = vector[..., :half]
    second = vector[..., half:]
    return jnp.concatenate(
        [first * cosine - second * sine, second * cosine + first * sine], axis=-1
    )


def dot_nt(a, b):
    return lax.dot_general(a, b, (((1,), (1,)), ((), ())), preferred_element_type=F32)


def dot_tn(a, b):
    return lax.dot_general(a, b, (((0,), (0,)), ((), ())), preferred_element_type=F32)


def body(
    scal, pdest, index, tab, meta, pack, pool_hbm, prompt_hbm, out,
    pool, pages, ab, mig_send, mig_rcv, ret_loc, ret_send, ret_rcv,
    qa, qb, acc, lse,
    sa, sb, la, lb, ra, rb, rla, rlb,
    sa2, sb2, la2, lb2, ra2, rb2, rla2, rlb2,
    s3, l3, r3, rl3, wgt, fin,
    local_sem, core_ssem, core_rsem, mig_ssem, mig_rsem, ret_ssem, ret_rsem,
    gz_ssem, gz_rsem, g2_ssem, g2_rsem, g3_ssem, g3_rsem,
    r1_ssem, r1_rsem, r2_ssem, r2_rsem, rz_ssem, rz_rsem,
):
    inst = lax.axis_index("inst")
    tp = lax.axis_index("tp")
    z_lo, y, x = inst // 16, (inst // 4) % 4, inst % 4
    z_hi, core = tp // 2, tp % 2
    z = z_hi * 4 + z_lo

    def device(zz, yy, xx, cc):
        return ((zz % 4) * 16 + yy * 4 + xx, (zz // 4) * 2 + cc)

    x_peers = [device(z, y, (x + k) % 4, core) for k in (1, 2, 3)]
    y_peers = [device(z, (y + k) % 4, x, core) for k in (1, 2, 3)]
    z_peers = [device((z + k) % 8, y, x, core) for k in range(1, 8)]
    core_peer = device(z, y, x, 1 - core)
    mig_peers = [
        device(z, y, x + 1 - 2 * (x % 2), core),
        device(z, y, (x + 2) % 4, core),
        device(z, y + 1 - 2 * (y % 2), x, core),
    ]

    barrier = pltpu.get_barrier_semaphore()
    everyone = [core_peer] + x_peers + y_peers + z_peers
    for peer in everyone:
        pl.semaphore_signal(barrier, inc=1, device_id=peer, device_id_type=MESH)

    def remote(src, dst, ssem, rsem, peer):
        return pltpu.make_async_remote_copy(
            src_ref=src, dst_ref=dst, send_sem=ssem, recv_sem=rsem,
            device_id=peer, device_id_type=MESH,
        )

    pool_copy = pltpu.make_async_copy(pool_hbm, pool, local_sem.at[0])
    pool_copy.start()
    own_copies = [
        pltpu.make_async_copy(
            prompt_hbm.at[:, :, pl.ds(hi * 4 + core * 2, 2)], pages.at[core, hi], local_sem.at[1 + hi]
        )
        for hi in range(2)
    ]
    for copy in own_copies:
        copy.start()

    my_slot = scal[0]
    bit = scal[1]
    mine = pack[4, pl.ds(0, 64)]
    qa[x, y, z] = mine[:32]
    qb[y, x, z] = mine[32:]
    mig_send[...] = pack[my_slot]

    pl.semaphore_wait(barrier, len(everyone))

    gz = []
    for k in range(7):
        gz.append(remote(qa.at[x, y, z], qa.at[x, y, z], gz_ssem.at[0, k], gz_rsem.at[0, k], z_peers[k]))
        gz.append(remote(qb.at[y, x, z], qb.at[y, x, z], gz_ssem.at[1, k], gz_rsem.at[1, k], z_peers[k]))
    for copy in gz:
        copy.start()
    mig = [remote(mig_send, mig_rcv.at[k], mig_ssem.at[k], mig_rsem.at[k], mig_peers[k]) for k in range(3)]
    for copy in mig:
        copy.start()
    core_copies = [
        remote(
            prompt_hbm.at[:, :, pl.ds(hi * 4 + (1 - core) * 2, 2)],
            pages.at[core, hi], core_ssem.at[hi], core_rsem.at[hi], core_peer,
        )
        for hi in range(2)
    ]
    for copy in core_copies:
        copy.start()

    shape = (12, 8, HD)
    row = lax.broadcasted_iota(jnp.int32, shape, 1)
    page_id = lax.broadcasted_iota(jnp.int32, shape, 0) * 4 + row % 4
    is_last = (row // 4).astype(jnp.int32)
    full = meta[pl.ds(0, 1), :]
    ab[...] = jnp.zeros(shape, F32)

    def count_step(k, carry):
        named = tab[pl.ds(k, 1), :][None]
        kind = jnp.where(k < full, 0, jnp.where(k == full, 1, 2))[None]
        hit = (page_id == named) & (is_last == kind)
        ab[...] += jnp.where(hit, 1.0, 0.0)
        return carry

    lax.fori_loop(0, 24, count_step, 0)

    for copy in gz:
        copy.wait()
    g2 = []
    for k in range(3):
        g2.append(remote(qa.at[x, y], qa.at[x, y], g2_ssem.at[0, k], g2_rsem.at[0, k], y_peers[k]))
        g2.append(remote(qb.at[y, x], qb.at[y, x], g2_ssem.at[1, k], g2_rsem.at[1, k], x_peers[k]))
    for copy in g2:
        copy.start()
    for copy in mig:
        copy.wait()
    for copy in g2:
        copy.wait()
    g3 = []
    for k in range(3):
        g3.append(remote(qa.at[x], qa.at[x], g3_ssem.at[0, k], g3_rsem.at[0, k], x_peers[k]))
        g3.append(remote(qb.at[y], qb.at[y], g3_ssem.at[1, k], g3_rsem.at[1, k], y_peers[k]))
    for copy in g3:
        copy.start()

    came = mig_rcv[bit].astype(F32)
    blocks = [jnp.where(my_slot == j, came, pack[j].astype(F32)).astype(BF16) for j in range(4)]
    fresh_kv = jnp.concatenate([block[64:80] for block in blocks], axis=0)
    q_res = [jnp.concatenate([block[h * 32 : h * 32 + 32] for block in blocks], axis=0) for h in range(2)]
    pool_copy.wait()
    rem = meta[pl.ds(1, 1), :]
    below = (lax.broadcasted_iota(jnp.int32, (64, HD), 0) < rem).astype(F32)

    def res_step(i, carry):
        named = ab[i]
        count = (named[0:4][:, None, :] + named[4:8][:, None, :] * below[None]).reshape(256, HD)
        real = count > 0.0
        after = []
        for h in range(2):
            best, total, summed = carry[3 * h : 3 * h + 3]
            keys = pool[pl.ds(i * 4, 4), 0, h].reshape(256, HD)
            values = pool[pl.ds(i * 4, 4), 1, h].reshape(256, HD)
            score = jnp.where(real, dot_nt(keys, q_res[h]) * SCALE, NEG)
            top = jnp.maximum(best, jnp.max(score, axis=0, keepdims=True))
            weight = (count * jnp.exp(score - top)).astype(BF16)
            shrink = jnp.exp(best - top)
            total = total * shrink + jnp.sum(weight.astype(F32), axis=0, keepdims=True)
            summed = summed * shrink + dot_tn(values, weight)
            after += [top, total, summed]
        return tuple(after)

    start = (jnp.full((1, HD), NEG, F32), jnp.zeros((1, HD), F32), jnp.zeros((HD, HD), F32)) * 2
    state = lax.fori_loop(0, 12, res_step, start)
    lane = lax.broadcasted_iota(jnp.int32, (64, HD), 1)
    line = lax.broadcasted_iota(jnp.int32, (64, HD), 0)
    ok_slot = (line // 16 == lane // 32) & (line % 16 < 8) & (line % 4 <= (lane % 32) // 8)
    rows = []
    for h in range(2):
        best, total, summed = state[3 * h : 3 * h + 3]
        ok = ok_slot & ((line % 8) // 4 == h)
        score = jnp.where(ok, dot_nt(fresh_kv, q_res[h]) * SCALE, NEG)
        top = jnp.maximum(best, jnp.max(score, axis=0, keepdims=True))
        weight = jnp.where(ok, jnp.exp(score - top), 0.0).astype(BF16).astype(F32)
        moved = jnp.concatenate([jnp.zeros((8, HD), F32), weight[:-8]], axis=0).astype(BF16)
        shrink = jnp.exp(best - top)
        total = total * shrink + jnp.sum(weight, axis=0, keepdims=True)
        summed = summed * shrink + dot_tn(fresh_kv, moved)
        rows.append((summed / total).T)
    for j in range(4):
        for s in range(4):
            at = j * 32 + s * 8
            ret_loc[j, s] = jnp.concatenate([rows[0][at : at + 8], rows[1][at : at + 8]], axis=0).astype(BF16)
    ret_send[...] = ret_loc[my_slot]
    ret = [remote(ret_send, ret_rcv.at[k], ret_ssem.at[k], ret_rsem.at[k], mig_peers[k]) for k in range(3)]
    for copy in ret:
        copy.start()

    for copy in own_copies + core_copies:
        copy.wait()
    for copy in g3:
        copy.wait()
    acc[24] = jnp.zeros((HD, HD), F32)
    lse[24] = jnp.full((1, HD), NEG, F32)
    key_head = lax.broadcasted_iota(jnp.int32, (256, HD), 0) // 64
    row_head = lax.broadcasted_iota(jnp.int32, (256, HD), 1) // 32
    same_head = key_head == row_head

    def query_of(d):
        zl, dy, dx = d // 16, (d // 4) % 4, d % 4
        return jnp.concatenate(
            [qa[dx, dy, zl], qb[dy, dx, zl], qa[dx, dy, zl + 4], qb[dy, dx, zl + 4]], axis=0
        )

    def page_step(i, carry):
        for src in range(2):
            n = src * 12 + i
            asked = query_of(pdest[n])
            keys = jnp.concatenate([pages[src, hi, i, 0].reshape(HD, HD) for hi in range(2)], axis=0)
            values = jnp.concatenate([pages[src, hi, i, 1].reshape(HD, HD) for hi in range(2)], axis=0)
            score = jnp.where(same_head, dot_nt(keys, asked) * SCALE, NEG)
            top = jnp.max(score, axis=0, keepdims=True)
            weight = jnp.exp(score - top).astype(BF16)
            total = jnp.sum(weight.astype(F32), axis=0, keepdims=True)
            acc[n] = dot_tn(values, weight) / total
            lse[n] = top + jnp.log(total)
        return carry

    lax.fori_loop(0, 12, page_step, 0)

    for dx in range(4):
        def place_step(t, carry, dx=dx):
            dy, zl = t // 4, t % 4
            d = zl * 16 + dy * 4 + dx
            first, second = index[0, d], index[1, d]
            lse0, lse1 = lse[first], lse[second]
            top = jnp.maximum(lse0, lse1)
            w0, w1 = jnp.exp(lse0 - top), jnp.exp(lse1 - top)
            total = w0 + w1
            both = top + jnp.log(total)
            block = acc[first] * (w0 / total) + acc[second] * (w1 / total)
            sa[dx, t] = block[:64].astype(BF16)
            sb[dy, dx * 4 + zl] = block[64:].astype(BF16)
            la[dx, pl.ds(t, 1), :] = both
            lb[dy, pl.ds(dx * 4 + zl, 1), :] = both
            return carry

        lax.fori_loop(0, 16, place_step, 0)

    r1 = []
    for k in range(3):
        to_x, to_y = (x + k + 1) % 4, (y + k + 1) % 4
        r1.append(remote(sa.at[to_x], ra.at[k], r1_ssem.at[0, k], r1_rsem.at[0, k], x_peers[k]))
        r1.append(remote(la.at[to_x], rla.at[k], r1_ssem.at[1, k], r1_rsem.at[1, k], x_peers[k]))
        r1.append(remote(sb.at[to_y], rb.at[k], r1_ssem.at[2, k], r1_rsem.at[2, k], y_peers[k]))
        r1.append(remote(lb.at[to_y], rlb.at[k], r1_ssem.at[3, k], r1_rsem.at[3, k], y_peers[k]))
    for copy in r1:
        copy.start()

    asked = query_of(inst)
    own_kv = pack[4, pl.ds(64, 16)]
    lane16 = lax.broadcasted_iota(jnp.int32, (16, HD), 1)
    line16 = lax.broadcasted_iota(jnp.int32, (16, HD), 0)
    ok = (line16 < 8) & (line16 // 4 == (lane16 % 64) // 32) & (line16 % 4 <= (lane16 % 32) // 8)
    score = jnp.where(ok, dot_nt(own_kv, asked) * SCALE, NEG)
    top = jnp.max(score, axis=0, keepdims=True)
    weight = jnp.where(ok, jnp.exp(score - top), 0.0).astype(BF16).astype(F32)
    moved = jnp.concatenate([jnp.zeros((8, HD), F32), weight[:-8]], axis=0).astype(BF16)
    total = jnp.sum(weight, axis=0, keepdims=True)
    new_acc = dot_tn(own_kv, moved) / total
    new_lse = top + jnp.log(total)

    def shares(parts):
        top = parts[0]
        for part in parts[1:]:
            top = jnp.maximum(top, part)
        weights = [jnp.exp(part - top) for part in parts]
        total = weights[0]
        for part in weights[1:]:
            total = total + part
        return [part / total for part in weights], top + jnp.log(total)

    for copy in r1:
        copy.wait()
    for side, (mine_s, mine_l, got_s, got_l, where, next_s, next_l) in enumerate((
        (sa, la, ra, rla, x, sa2, la2), (sb, lb, rb, rlb, y, sb2, lb2)
    )):
        weights, joined = shares([mine_l[where]] + [got_l[k] for k in range(3)])
        for k in range(4):
            wgt[k] = weights[k]
        for group in range(4):
            next_l[group] = jnp.concatenate([joined[group * 4 : group * 4 + 4], jnp.zeros((4, HD), F32)], axis=0)

        def merge_step(t, carry):
            block = mine_s[where, t].astype(F32) * wgt[0, pl.ds(t, 1), :]
            for k in range(3):
                block = block + got_s[k, t].astype(F32) * wgt[k + 1, pl.ds(t, 1), :]
            next_s[t // 4, t % 4] = block.astype(BF16)
            return carry

        lax.fori_loop(0, 16, merge_step, 0)

    r2 = []
    for k in range(3):
        to_x, to_y = (x + k + 1) % 4, (y + k + 1) % 4
        r2.append(remote(sa2.at[to_y], ra2.at[k], r2_ssem.at[0, k], r2_rsem.at[0, k], y_peers[k]))
        r2.append(remote(la2.at[to_y], rla2.at[k], r2_ssem.at[1, k], r2_rsem.at[1, k], y_peers[k]))
        r2.append(remote(sb2.at[to_x], rb2.at[k], r2_ssem.at[2, k], r2_rsem.at[2, k], x_peers[k]))
        r2.append(remote(lb2.at[to_x], rlb2.at[k], r2_ssem.at[3, k], r2_rsem.at[3, k], x_peers[k]))
    for copy in r2:
        copy.start()
    for copy in ret:
        copy.wait()
    back = [ret_rcv[bit, s].astype(F32) for s in range(4)]
    for j in range(4):
        for s in range(4):
            out[j, s] = jnp.where(my_slot == j, back[s], ret_loc[j, s].astype(F32)).astype(BF16)
    for copy in r2:
        copy.wait()
    joins = []
    for side, (mine_s, mine_l, got_s, got_l, where) in enumerate((
        (sa2, la2, ra2, rla2, y), (sb2, lb2, rb2, rlb2, x)
    )):
        weights, joined = shares([mine_l[where]] + [got_l[k] for k in range(3)])
        joins.append(joined)
        for zl in range(4):
            block = mine_s[where, zl].astype(F32) * weights[0][zl : zl + 1]
            for k in range(3):
                block = block + got_s[k, zl].astype(F32) * weights[k + 1][zl : zl + 1]
            s3[zl, pl.ds(side * 64, 64)] = block.astype(BF16)
    for zl in range(4):
        l3[zl] = jnp.concatenate(
            [joins[0][zl : zl + 1], joins[1][zl : zl + 1], jnp.zeros((6, HD), F32)], axis=0
        )
    rz = []
    for k in range(7):
        to = (z + k + 1) % 4
        rz.append(remote(s3.at[to], r3.at[k], rz_ssem.at[0, k], rz_rsem.at[0, k], z_peers[k]))
        rz.append(remote(l3.at[to], rl3.at[k], rz_ssem.at[1, k], rz_rsem.at[1, k], z_peers[k]))
    for copy in rz:
        copy.start()
    for copy in rz:
        copy.wait()
    new_rows = jnp.concatenate([new_lse] * 8, axis=0)
    weights, _ = shares([new_rows, l3[z_lo]] + [rl3[k] for k in range(7)])
    halves = []
    for side in range(2):
        at = pl.ds(side * 64, 64)
        block = new_acc[side * 64 : side * 64 + 64] * weights[0][side : side + 1]
        block = block + s3[z_lo, at].astype(F32) * weights[1][side : side + 1]
        for k in range(7):
            block = block + r3[k, at].astype(F32) * weights[k + 2][side : side + 1]
        halves.append(block)
    fin[...] = jnp.concatenate(halves, axis=0).T
    here = fin[pl.ds(z_hi * 64, 64), :]
    for s in range(4):
        out[4, s] = jnp.concatenate([here[s * 8 : s * 8 + 8], here[32 + s * 8 : 40 + s * 8]], axis=0).astype(BF16)


def per_device(
    pool_kv, block_table, context_len, partner, mig_slot, prompt_kv, prompt_dest, queries, step_kv
):
    inst = lax.axis_index("inst")
    tp = lax.axis_index("tp")
    my_slot = mig_slot[inst]
    mate = partner[inst]
    mate_len = context_len[mate, mig_slot[mate]]
    own_len = context_len[inst]
    post_len = jnp.where(jnp.arange(4, dtype=jnp.int32) == my_slot, mate_len, own_len)
    dests = prompt_dest[:, 0]
    new_len = jnp.sum((dests == inst).astype(jnp.int32)) * 64
    lens = jnp.concatenate([post_len, new_len[None]])
    positions = lens[:, None] + jnp.arange(4, dtype=jnp.int32)
    angles = positions.astype(F32)[..., None] * rope_freqs(HD)
    cosine, sine = jnp.cos(angles)[:, :, None], jnp.sin(angles)[:, :, None]
    qrot = rotate(queries.astype(F32), cosine, sine).astype(BF16)
    qrot = qrot.reshape(5, 4, 2, 8, HD).transpose(0, 2, 1, 3, 4).reshape(5, 64, HD)
    knew = rotate(step_kv[:, :, 0].astype(F32), cosine, sine).astype(BF16)
    knew = knew.transpose(0, 2, 1, 3).reshape(5, 8, HD)
    vnew = step_kv[:, :, 1].transpose(0, 2, 1, 3).reshape(5, 8, HD)
    pack = jnp.concatenate([qrot, knew, vnew], axis=1)

    gap = jnp.bitwise_xor(inst, mate)
    bit = jnp.where(gap == 1, 0, jnp.where(gap == 2, 1, 2))
    scal = jnp.stack([my_slot, bit]).astype(jnp.int32)
    tab = jnp.repeat(block_table.T, 32, axis=1)
    lanes = jnp.repeat(own_len, 32)
    meta = jnp.concatenate([(lanes // 64)[None], (lanes % 64)[None], jnp.zeros((6, HD), jnp.int32)])
    pdest = lax.dynamic_slice_in_dim(dests, inst * 48 + (tp // 2) * 24, 24)
    order = jnp.arange(24, dtype=jnp.int32)
    match = pdest[None, :] == jnp.arange(64, dtype=jnp.int32)[:, None]
    first = jnp.min(jnp.where(match, order, 24), axis=1)
    last = jnp.max(jnp.where(match, order, -1), axis=1)
    index = jnp.stack([first, jnp.where(last > first, last, 24)])

    smem = pl.BlockSpec(memory_space=pltpu.SMEM)
    vmem = pl.BlockSpec(memory_space=pltpu.VMEM)
    hbm = pl.BlockSpec(memory_space=pl.ANY)
    sem = lambda *shape: pltpu.SemaphoreType.DMA(shape)
    V = pltpu.VMEM
    return pl.pallas_call(
        body,
        out_shape=jax.ShapeDtypeStruct((5, 4, 16, HD), BF16),
        in_specs=[smem, smem, smem, vmem, vmem, vmem, hbm, hbm],
        out_specs=vmem,
        scratch_shapes=[
            V((48, 2, 2, 64, HD), BF16),
            V((2, 2, 12, 2, 2, 64, HD), BF16),
            V((12, 8, HD), F32),
            V((80, HD), BF16),
            V((3, 80, HD), BF16),
            V((4, 4, 16, HD), BF16),
            V((4, 16, HD), BF16),
            V((3, 4, 16, HD), BF16),
            V((4, 4, 8, 32, HD), BF16),
            V((4, 4, 8, 32, HD), BF16),
            V((25, HD, HD), F32),
            V((25, 1, HD), F32),
            V((4, 16, 64, HD), BF16),
            V((4, 16, 64, HD), BF16),
            V((4, 16, HD), F32),
            V((4, 16, HD), F32),
            V((3, 16, 64, HD), BF16),
            V((3, 16, 64, HD), BF16),
            V((3, 16, HD), F32),
            V((3, 16, HD), F32),
            V((4, 4, 64, HD), BF16),
            V((4, 4, 64, HD), BF16),
            V((4, 8, HD), F32),
            V((4, 8, HD), F32),
            V((3, 4, 64, HD), BF16),
            V((3, 4, 64, HD), BF16),
            V((3, 8, HD), F32),
            V((3, 8, HD), F32),
            V((4, HD, HD), BF16),
            V((4, 8, HD), F32),
            V((7, HD, HD), BF16),
            V((7, 8, HD), F32),
            V((4, 16, HD), F32),
            V((HD, HD), F32),
            sem(3), sem(2), sem(2), sem(3), sem(3), sem(3), sem(3),
            sem(2, 7), sem(2, 7), sem(2, 3), sem(2, 3), sem(2, 3), sem(2, 3),
            sem(4, 3), sem(4, 3), sem(4, 3), sem(4, 3), sem(2, 7), sem(2, 7),
        ],
        compiler_params=pltpu.CompilerParams(
            collective_id=0, has_side_effects=True, vmem_limit_bytes=48 * 1024 * 1024
        ),
    )(scal, pdest, index, tab, meta, pack, pool_kv, prompt_kv)


def solution(mesh):
    placed = (
        P("inst", None, "tp", None, None),
        P("inst", None),
        P(),
        P(),
        P(),
        P(("inst", "tp"), None, None, None, None),
        P(),
        P("inst", None, "tp", None),
        P("inst", None, None, "tp", None),
    )
    return jax.shard_map(
        per_device,
        mesh=mesh,
        in_specs=placed,
        out_specs=P("inst", None, "tp", None),
        check_vma=False,
    )
```

time: 360 us -> 91.2 us (0.25); the launches traced: 354 us -> 90.5 us
  waiting for transfers between devices: 204 us -> 0 us
  Pallas kernels: 0 us -> 70.3 us
  local copies, waits for them, and re-layouts: 48 us -> 9.24 us
  starting transfers between devices: 38 us -> 0 us
  other arithmetic: 35.8 us -> 5.95 us
  matrix products: 19.7 us -> 0 us
  between operations: 8.8 us -> 4.99 us
    ppermute x3 -> x0, waiting for transfers between devices: 147 us -> none  [swapped(): return lax.ppermute(value, axis, pairs)]
    pallas_call x0 -> x1, Pallas kernels: none -> 70.3 us  [per_device(): pl.pallas_call(body, out_shape=jax.ShapeDtypeStruct((5, 4, 16, HD), BF16)...]
    all_to_all x2 -> x0, waiting for transfers between devices: 57 us -> none  [the longest x1 57 us: per_device(): lax.all_to_all(prompt_kv, 'tp', split_axis=2, concat_axis=0, tiled=True)]
    all_to_all x2 -> x0, starting transfers between devices: 33 us -> none  [the longest x1 24.4 us: per_device(): lax.all_to_all(outbox, 'inst', split_axis=0, concat_axis=0, tiled=True)]
    select_n x7 -> x3, other arithmetic: 27.7 us -> 1.27 us  [the longest x1 1.25 us: per_device(): jnp.where(jnp.arange(4, dtype=jnp.int32) == my_slot, mate_len, own_len)]
    dot_general x8 -> x0, matrix products: 19.7 us -> none  [the longest x4 12.4 us: page_stats(): jnp.einsum('hrpt,phtd->hrpd', weights, values, preferred_element_type=jnp...]
    gather x3 -> x0, local copies, waits for them, and re-layouts: 16.2 us -> none  [the longest x1 8.3 us: per_device(): mine_pages[source]]
    all_to_all x2 -> x0, local copies, waits for them, and re-layouts: 13.9 us -> none  [the longest x1 9.33 us: per_device(): lax.all_to_all(outbox, 'inst', split_axis=0, concat_axis=0, tiled=True)]
  transfers between devices with their start and end apart: 5 -> 0, of which waited for: 4 -> 0; matrix products, arithmetic and copies ran while one was open for 11% -> 0% of each run, Pallas kernels for 0% -> 0%
where the time goes in v1:
time: 91.2 us; the launch traced here: 90.5 us
  Pallas kernels  70.3 us (77%)
  local copies, waits for them, and re-layouts  9.24 us (10%)
  other arithmetic  5.95 us (7%)
  between operations  4.99 us (5%)
    pallas_call x1, Pallas kernels, per_device(): pl.pallas_call(body, out_shape=jax.ShapeDtypeStruct((5, 4, 16, HD), BF16)...  70.3 us
    dynamic_slice x2, local copies, waits for them, and re-layouts, per_device(): mate_len = context_len[mate, mig_slot[mate]]  2.67 us
    unnamed x3, local copies, waits for them, and re-layouts  2.53 us

profile of v1, /device:TPU:2, one launch (start us, length us, event | category | flops | bytes accessed | tf_op | source)
XLA Modules:
  0.0 90.5 jit_solution(6999823524202181242)
XLA Ops:
  0.0 1.2 %dynamic_slice.21 = s32[1]{0:T(128)} dynamic-slice(s32[64]{0:T(128)} %param.12, s32[]{:T(128)S(6)} %select_n.90), dynamic_slice_sizes={1} | dynamic-slice | bytes 12 | tf_op jit(solution)/shard_map/dynamic_slice | solution.py:379
  3.2 1.4 %fusion.3 = (s32[1]{0:T(128)}, s32[1]{0:T(128)}) fusion(s32[64]{0:T(128)} %param.13, s32[]{:T(128)S(6)} %select_n.100, s32[]{:T(128)S(6)} %select_n.90), kind=kLoop, calls=%fused_computation.34 | loop fusion | bytes 24 | tf_op jit(solution)/shard_map/dynamic_slice | solution.py:380
  6.3 1.3 %dynamic_slice.26 = s32[1,1]{0,1:T(1,128)} dynamic-slice(s32[64,4]{0,1:T(4,128)} %param.11, s32[]{:T(128)S(6)} %select_n.100, s32[]{:T(128)S(6)} %select_n.101), dynamic_slice_sizes={1,1} | dynamic-slice | bytes 12 | tf_op jit(solution)/shard_map/dynamic_slice | solution.py:380
  7.5 0.9 dynamic-slice_reduce_fusion
  8.4 1.3 %compare_select_fusion.3 = s32[4]{0:T(128)S(1)} fusion(s32[4]{0:T(128)S(1)} %dynamic-slice_reduce_fusion, s32[]{:T(128)} %bitcast.8, s32[]{:T(128)} %bitcast.6), kind=kLoop, calls=%fused_computation.24 | loop fusion | flops 8 | bytes 40 | tf_op jit(solution)/shard_map/jit(_where)/select_n | solution.py:382
  9.7 1.4 %fusion.2 = s32[]{:T(128)} fusion(s32[3072,1]{0,1:T(1,128)} %param.15, s32[]{:T(128)S(6)} %axis_index.23), kind=kLoop, calls=%fused_computation.11 | loop fusion | flops 9215 | bytes 12296 | tf_op jit(solution)/shard_map/reduce_sum | solution.py:384
  11.6 0.1 pad_add_fusion.2
  11.7 0.1 add_convert_fusion.2
  11.8 0.2 multiply_cosine_fusion
  11.9 0.9 convert_element_type.23
  12.8 0.1 fusion
  13.0 0.1 pad_maximum_fusion.1
  13.1 0.7 bitcast_convert_fusion
  13.8 0.1 subtract_convert_fusion.1
  13.9 0.1 maximum_bitcast_fusion
  14.1 0.8 dynamic-slice_bitcast_fusion.pdest
  14.8 0.1 select_reduce_fusion.1
  15.6 0.8 pad_add_fusion.1.scal
  16.4 0.1 broadcast_in_dim.50
  16.4 0.1 reshape.192
  16.6 0.1 pad.11.clone
  16.6 0.1 add_add_fusion.meta
  16.7 0.8 copy.15
  17.5 0.1 broadcast_in_dim.49
  17.5 0.1 reshape.191.tab
  17.6 0.0 copy-start
  17.7 1.9 %copy-done = bf16[48,2,2,64,128]{4,3,2,1,0:T(8,128)(2,1)S(1)} copy-done((bf16[48,2,2,64,128]{4,3,2,1,0:T(8,128)(2,1)S(1)}, bf16[48,2,2,64,128]{4,3,2,1,0:T(8,128)(2,1)}, u32[]{:S(2)}) %copy-start) | copy-done | bytes 3145752
  19.5 70.3 %shard_map.91 = bf16[5,4,16,128]{3,2,1,0:T(8,128)(2,1)S(1)} custom-call(s32[2]{0:T(128)S(1)} %pad_add_fusion.1.scal, s32[24]{0:T(128)S(1)} %dynamic-slice_bitcast_fusion.pdest, s32[2,64]{1,0:T(2,128)S(1)} %pad_add_fusion.index, s32[24,128]{1,0:T(8,128)S(1)} %reshape.191.tab, s32[8,128]{1,0:T(8,128)S(1)} %add_add_fusion.meta, ...), custom_call_target="tpu_custom_call" | custom-call | tf_op jit(solution)/shard_map/pallas_call | solution.py:414
  89.9 0.6 copy.22
  (9 shorter events, 0.1 us)
Async XLA Ops:
  17.6 1.9 %copy-start = (bf16[48,2,2,64,128]{4,3,2,1,0:T(8,128)(2,1)S(1)}, bf16[48,2,2,64,128]{4,3,2,1,0:T(8,128)(2,1)}, u32[]{:S(2)}) copy-start(bf16[48,2,2,64,128]{4,3,2,1,0:T(8,128)(2,1)} %pool_hbm.1) | copy-start | bytes 9437188

commit v2 on v1

v2 whole, which is shorter than its diff:
```python
import math

import jax
import jax.numpy as jnp
import numpy as np
from jax import lax
from jax.experimental import pallas as pl
from jax.experimental.pallas import tpu as pltpu
from jax.sharding import PartitionSpec as P

MESH = pl.DeviceIdType.MESH
NEG = -1e30
F32 = jnp.float32
BF16 = jnp.bfloat16
HD = 128
SCALE = 1.0 / math.sqrt(HD)
UNROLL = 3


def rope_row():
    ratio = np.arange(HD // 2) * (2.0 / HD)
    base = np.exp(-ratio * math.log(500000.0))
    wavelength = 2.0 * math.pi / base
    smooth = (8192.0 / wavelength - 1.0) / 3.0
    blended = (1.0 - smooth) * base / 8.0 + smooth * base
    freqs = np.where(wavelength < 2048.0, base, np.where(wavelength > 8192.0, base / 8.0, blended))
    return np.concatenate([freqs, freqs])[None].astype(np.float32)


def cos_sin(angle):
    turns = jnp.floor(angle * (2.0 / math.pi) + 0.5)
    r = angle - turns * 1.5703125
    r = r - turns * 4.837512969970703125e-4
    r = r - turns * 7.54978995489188216e-8
    sq = r * r
    sine = ((-1.9515295891e-4 * sq + 8.3321608736e-3) * sq - 1.6666654611e-1) * sq * r + r
    cosine = (2.443315711809948e-5 * sq - 1.388731625493765e-3) * sq + 4.166664568298827e-2
    cosine = cosine * sq * sq - 0.5 * sq + 1.0
    quarter = turns - 4.0 * jnp.floor(turns * 0.25)
    odd = (quarter == 1.0) | (quarter == 3.0)
    first, second = jnp.where(odd, sine, cosine), jnp.where(odd, cosine, sine)
    first = jnp.where((quarter == 1.0) | (quarter == 2.0), -first, first)
    second = jnp.where(quarter >= 2.0, -second, second)
    return first, second


def dot_nt(a, b):
    return lax.dot_general(a, b, (((1,), (1,)), ((), ())), preferred_element_type=F32)


def dot_tn(a, b):
    return lax.dot_general(a, b, (((0,), (0,)), ((), ())), preferred_element_type=F32)


def shares(parts):
    top = parts[0]
    for part in parts[1:]:
        top = jnp.maximum(top, part)
    weights = [jnp.exp(part - top) for part in parts]
    total = weights[0]
    for part in weights[1:]:
        total = total + part
    return [part / total for part in weights], top + jnp.log(total)


def iota(shape, axis):
    return lax.broadcasted_iota(jnp.int32, shape, axis)


def body(
    dests, lengths, partner, mig_slot, table, dest_grid, freqs, queries, step_kv, pool_hbm, prompt_hbm, out,
    pool, pages, ab, index_v, index, mig_mine, mig_send, mig_rcv, ret_loc, ret_send, ret_rcv,
    zqa, zqb, qa_low, qa_high, qb_low, qb_high, acc, lse, acc2, lse2,
    sa, sb, la, lb, ra, rb, rla, rlb,
    sa2, sb2, la2, lb2, ra2, rb2, rla2, rlb2,
    s3, l3, r3, rl3,
    local_sem, core_ssem, core_rsem, mig_ssem, mig_rsem, ret_ssem, ret_rsem,
    gz_ssem, gz_rsem, g2_ssem, g2_rsem, g3_ssem, g3_rsem,
    r1_ssem, r1_rsem, r2_ssem, r2_rsem, rz_ssem, rz_rsem,
):
    inst = lax.axis_index("inst")
    tp = lax.axis_index("tp")
    z_lo, y, x = inst // 16, (inst // 4) % 4, inst % 4
    z_hi, core = tp // 2, tp % 2
    z = z_hi * 4 + z_lo

    def device(zz, yy, xx, cc):
        return ((zz % 4) * 16 + yy * 4 + xx, (zz // 4) * 2 + cc)

    x_peers = [device(z, y, (x + k) % 4, core) for k in (1, 2, 3)]
    y_peers = [device(z, (y + k) % 4, x, core) for k in (1, 2, 3)]
    z_peers = [device((z + k) % 8, y, x, core) for k in range(1, 8)]
    core_peer = device(z, y, x, 1 - core)
    mig_peers = [
        device(z, y, x + 1 - 2 * (x % 2), core),
        device(z, y, (x + 2) % 4, core),
        device(z, y + 1 - 2 * (y % 2), x, core),
    ]

    barrier = pltpu.get_barrier_semaphore()
    everyone = [core_peer] + x_peers + y_peers + z_peers
    for peer in everyone:
        pl.semaphore_signal(barrier, inc=1, device_id=peer, device_id_type=MESH)

    def remote(src, dst, ssem, rsem, peer):
        return pltpu.make_async_remote_copy(
            src_ref=src, dst_ref=dst, send_sem=ssem, recv_sem=rsem,
            device_id=peer, device_id_type=MESH,
        )

    pool_copy = pltpu.make_async_copy(pool_hbm, pool, local_sem.at[0])
    pool_copy.start()
    own_copies = [
        pltpu.make_async_copy(
            prompt_hbm.at[:, :, pl.ds(hi * 4 + core * 2, 2)], pages.at[core, hi], local_sem.at[1 + hi]
        )
        for hi in range(2)
    ]
    for copy in own_copies:
        copy.start()

    my_slot = mig_slot[inst]
    mate = partner[inst]
    mate_len = lengths[mig_slot[mate], mate]
    own_len = [lengths[j, inst] for j in range(4)]
    bit = jnp.where(mate // 4 != inst // 4, 2, jnp.where(mate // 2 != inst // 2, 1, 0))
    first_row = inst * 48 + z_hi * 24

    freq = freqs[...]
    lane8 = iota((8, HD), 1)
    line8 = iota((8, HD), 0)
    line16 = iota((16, HD), 0)
    sign = jnp.where(lane8[:1] < 64, -1.0, 1.0)
    is_key = (line16 // 2) % 2 == 0

    def tables(length):
        at = length + (line8 % 4).astype(F32)
        cosine, sine = cos_sin(at * freq)
        return cosine, sine * sign

    def key_tables(length):
        at = jnp.where(is_key, length + (line16 // 4).astype(F32), 0.0)
        cosine, sine = cos_sin(at * freq)
        return cosine, sine * sign

    def turn(value, cosine, sine):
        return value * cosine + pltpu.roll(value, 64, 1) * sine

    def turned_query(slot, cosine, sine):
        tiles = [[None] * 4, [None] * 4]
        for s in range(4):
            both = queries[slot, s].astype(F32)
            for h in range(2):
                tiles[h][s] = turn(both[h * 8 : h * 8 + 8], cosine[s : s + 1], sine[s : s + 1])
        return [jnp.concatenate(part, axis=0).astype(BF16) for part in tiles]

    named_here = jnp.where(dest_grid[...] == inst, 1.0, 0.0)
    new_len = jnp.sum(jnp.sum(named_here, axis=0, keepdims=True), axis=1, keepdims=True) * 64.0
    mine = turned_query(4, *tables(new_len))
    zqa[z] = mine[0]
    zqb[z] = mine[1]
    qa, qb = (qa_low, qa_high), (qb_low, qb_high)

    pl.semaphore_wait(barrier, len(everyone))

    gz = []
    for k in range(7):
        here = zqa.at[z]
        gz.append(remote(here, here, gz_ssem.at[0, k], gz_rsem.at[0, k], z_peers[k]))
        here = zqb.at[z]
        gz.append(remote(here, here, gz_ssem.at[1, k], gz_rsem.at[1, k], z_peers[k]))
    for copy in gz:
        copy.start()

    for j in range(4):
        length = jnp.where(my_slot == j, mate_len, own_len[j]).astype(F32)
        part = turned_query(j, *tables(length))
        mig_mine[j, pl.ds(0, 32)] = part[0]
        mig_mine[j, pl.ds(32, 32)] = part[1]
        mig_mine[j, pl.ds(64, 16)] = turn(step_kv[j].astype(F32), *key_tables(length)).astype(BF16)
    mig_send[...] = mig_mine[my_slot]
    mig = [remote(mig_send, mig_rcv.at[k], mig_ssem.at[k], mig_rsem.at[k], mig_peers[k]) for k in range(3)]
    for copy in mig:
        copy.start()
    core_copies = [
        remote(
            prompt_hbm.at[:, :, pl.ds(hi * 4 + (1 - core) * 2, 2)],
            pages.at[core, hi], core_ssem.at[hi], core_rsem.at[hi], core_peer,
        )
        for hi in range(2)
    ]
    for copy in core_copies:
        copy.start()

    first = jnp.full((8, HD), 24, jnp.int32)
    second = jnp.full((8, HD), 24, jnp.int32)
    for n in range(24):
        hit = lane8 == dests[first_row + n]
        second = jnp.where(hit & (first < 24), n, second)
        first = jnp.where(hit & (first == 24), n, first)
    index_v[...] = jnp.where(line8 == 0, first, second)
    index_copy = pltpu.make_async_copy(index_v, index, local_sem.at[3])
    index_copy.start()

    twice = jnp.concatenate(mine + mine, axis=0)
    own_kv = turn(step_kv[4].astype(F32), *key_tables(new_len)).astype(BF16)
    lane16 = iota((16, HD), 1)
    ok = is_key & (line16 % 2 == (lane16 % 64) // 32) & (line16 // 4 <= (lane16 % 32) // 8)
    score = jnp.where(ok, dot_nt(own_kv, twice) * SCALE, NEG)
    top = jnp.max(score, axis=0, keepdims=True)
    weight = jnp.where(ok, jnp.exp(score - top), 0.0).astype(BF16).astype(F32)
    total = jnp.sum(weight, axis=0, keepdims=True)
    new_acc = dot_tn(own_kv, pltpu.roll(weight, 2, 0).astype(BF16)) / total
    new_acc = jnp.where(iota((64, HD), 1) < 64, new_acc[:64], new_acc[64:])
    new_lse = top + jnp.log(total)

    shape = (12, 8, HD)
    row = iota(shape, 1)
    page_id = iota(shape, 0) * 4 + row % 4
    is_last = row // 4
    lane1 = lane8[:1]

    def by_slot(values):
        return jnp.where(
            lane1 < 64, jnp.where(lane1 < 32, values[0], values[1]), jnp.where(lane1 < 96, values[2], values[3])
        )

    context = by_slot(own_len)
    full, rem = context // 64, context % 64
    ab[...] = jnp.zeros(shape, F32)

    def count_step(k, carry):
        named = by_slot([table[j, k] for j in range(4)])[None]
        kind = jnp.where(k < full, 0, jnp.where(k == full, 1, 2))[None]
        hit = (page_id == named) & (is_last == kind)
        ab[...] += jnp.where(hit, 1.0, 0.0)
        return carry

    lax.fori_loop(0, 24, count_step, 0)

    for copy in gz:
        copy.wait()
    g2 = []
    for hi in range(2):
        for k in range(3):
            here = zqa.at[pl.ds(hi * 4, 4)]
            g2.append(remote(here, qa[hi].at[x, y], g2_ssem.at[hi, 0, k], g2_rsem.at[hi, 0, k], y_peers[k]))
            here = zqb.at[pl.ds(hi * 4, 4)]
            g2.append(remote(here, qb[hi].at[y, x], g2_ssem.at[hi, 1, k], g2_rsem.at[hi, 1, k], x_peers[k]))
    for copy in g2:
        copy.start()
    for hi in range(2):
        qa[hi][x, y] = zqa[pl.ds(hi * 4, 4)]
        qb[hi][y, x] = zqb[pl.ds(hi * 4, 4)]
    for copy in mig:
        copy.wait()

    came = mig_rcv[bit].astype(F32)
    blocks = [jnp.where(my_slot == j, came, mig_mine[j].astype(F32)).astype(BF16) for j in range(4)]
    fresh_kv = jnp.concatenate([block[64:80] for block in blocks], axis=0)
    q_res = [jnp.concatenate([block[h * 32 : h * 32 + 32] for block in blocks], axis=0) for h in range(2)]
    pool_copy.wait()
    below = (iota((64, HD), 0) < rem).astype(F32)

    def res_step(i, carry):
        named = ab[i]
        count = (named[0:4][:, None, :] + named[4:8][:, None, :] * below[None]).reshape(256, HD)
        real = count > 0.0
        after = []
        for h in range(2):
            best, total, summed = carry[3 * h : 3 * h + 3]
            keys = pool[pl.ds(i * 4, 4), 0, h].reshape(256, HD)
            values = pool[pl.ds(i * 4, 4), 1, h].reshape(256, HD)
            score = jnp.where(real, dot_nt(keys, q_res[h]) * SCALE, NEG)
            top = jnp.maximum(best, jnp.max(score, axis=0, keepdims=True))
            weight = (count * jnp.exp(score - top)).astype(BF16)
            shrink = jnp.exp(best - top)
            total = total * shrink + jnp.sum(weight.astype(F32), axis=0, keepdims=True)
            summed = summed * shrink + dot_tn(values, weight)
            after += [top, total, summed]
        return tuple(after)

    start = (jnp.full((1, HD), NEG, F32), jnp.zeros((1, HD), F32), jnp.zeros((HD, HD), F32)) * 2
    state = lax.fori_loop(0, 4, res_step, start)
    for copy in g2:
        copy.wait()
    g3 = [[], []]
    for hi in range(2):
        for k in range(3):
            here = qa[hi].at[x]
            g3[hi].append(remote(here, here, g3_ssem.at[hi, 0, k], g3_rsem.at[hi, 0, k], x_peers[k]))
            here = qb[hi].at[y]
            g3[hi].append(remote(here, here, g3_ssem.at[hi, 1, k], g3_rsem.at[hi, 1, k], y_peers[k]))
        for copy in g3[hi]:
            copy.start()

    state = lax.fori_loop(4, 12, res_step, state)
    lane = iota((64, HD), 1)
    line = iota((64, HD), 0)
    ok_slot = (line // 16 == lane // 32) & ((line // 2) % 2 == 0) & ((line % 16) // 4 <= (lane % 32) // 8)
    rows = []
    for h in range(2):
        best, total, summed = state[3 * h : 3 * h + 3]
        ok = ok_slot & (line % 2 == h)
        score = jnp.where(ok, dot_nt(fresh_kv, q_res[h]) * SCALE, NEG)
        top = jnp.maximum(best, jnp.max(score, axis=0, keepdims=True))
        weight = jnp.where(ok, jnp.exp(score - top), 0.0).astype(BF16).astype(F32)
        shrink = jnp.exp(best - top)
        total = total * shrink + jnp.sum(weight, axis=0, keepdims=True)
        summed = summed * shrink + dot_tn(fresh_kv, pltpu.roll(weight, 2, 0).astype(BF16))
        rows.append((summed / total).T)
    for j in range(4):
        for s in range(4):
            at = j * 32 + s * 8
            ret_loc[j, s] = jnp.concatenate([rows[0][at : at + 8], rows[1][at : at + 8]], axis=0).astype(BF16)
    ret_send[...] = ret_loc[my_slot]
    ret = [remote(ret_send, ret_rcv.at[k], ret_ssem.at[k], ret_rsem.at[k], mig_peers[k]) for k in range(3)]
    for copy in ret:
        copy.start()

    for copy in own_copies + core_copies:
        copy.wait()
    index_copy.wait()
    acc[24] = jnp.zeros((HD, HD), F32)
    acc2[24] = jnp.zeros((HD, HD), F32)
    lse[24] = jnp.full((1, HD), NEG, F32)
    lse2[24] = jnp.full((1, HD), NEG, F32)
    same_head = iota((HD, HD), 0) // 64 == (iota((HD, HD), 1) % 64) // 32
    left = iota((HD, HD), 1) < 64
    left1 = lane1 < 64
    zeros6 = jnp.zeros((6, HD), F32)

    def prompt_part(hi):
        def page(n, src, i):
            d = dests[first_row + n]
            zl, dy, dx = d // 16, (d // 4) % 4, d % 4
            half = [qa[hi][dx, dy, zl], qb[hi][dy, dx, zl]]
            asked = jnp.concatenate(half + half, axis=0)
            score = jnp.where(same_head, dot_nt(pages[src, hi, i, 0].reshape(HD, HD), asked) * SCALE, NEG)
            top = jnp.max(score, axis=0, keepdims=True)
            weight = jnp.exp(score - top).astype(BF16)
            total = jnp.sum(weight.astype(F32), axis=0, keepdims=True)
            acc[n] = dot_tn(pages[src, hi, i, 1].reshape(HD, HD), weight) / total
            lse[n] = top + jnp.log(total)

        def page_step(i, carry):
            for src in range(2):
                for more in range(UNROLL):
                    page(src * 12 + i * UNROLL + more, src, i * UNROLL + more)
            return carry

        lax.fori_loop(0, 12 // UNROLL, page_step, 0)

        def join_step(i, carry):
            for more in range(4):
                n = i * 4 + more
                d = dests[first_row + n]
                first = index[0, d]
                other = jnp.where(first == n, index[1, d], first)
                weights, joined = shares([lse[n], lse[other]])
                acc2[n] = acc[n] * weights[0] + acc[other] * weights[1]
                lse2[n] = joined
            return carry

        lax.fori_loop(0, 6, join_step, 0)

        for zp in range(2):
            def place_step(dy, carry):
                for dx in range(4):
                    d = zp * 32 + dy * 4 + dx
                    one, two = index[0, d], index[0, d + 16]
                    block = jnp.where(left, acc2[one], acc2[two]).astype(BF16)
                    stat = jnp.where(left1, lse2[one], lse2[two])
                    sa[hi, dx, dy * 2 + zp] = block[:64]
                    sb[hi, dy, dx * 2 + zp] = block[64:]
                    la[hi, dx, pl.ds(dy * 2 + zp, 1), :] = stat
                    lb[hi, dy, pl.ds(dx * 2 + zp, 1), :] = stat
                return carry

            lax.fori_loop(0, 4, place_step, 0)

    def send_first(hi):
        sent = []
        for k in range(3):
            to_x, to_y = (x + k + 1) % 4, (y + k + 1) % 4
            for m, (src, dst, peer) in enumerate((
                (sa.at[hi, to_x], ra.at[hi, k], x_peers[k]),
                (sb.at[hi, to_y], rb.at[hi, k], y_peers[k]),
                (la.at[hi, to_x], rla.at[hi, k], x_peers[k]),
                (lb.at[hi, to_y], rlb.at[hi, k], y_peers[k]),
            )):
                sent.append(remote(src, dst, r1_ssem.at[hi, m, k], r1_rsem.at[hi, m, k], peer))
        for copy in sent:
            copy.start()
        return sent

    def merge_first(hi):
        for mine_s, mine_l, got_s, got_l, where, next_s, next_l in (
            (sa, la, ra, rla, x, sa2, la2), (sb, lb, rb, rlb, y, sb2, lb2)
        ):
            weights, joined = shares([mine_l[hi, where]] + [got_l[hi, k] for k in range(3)])
            for t in range(8):
                block = mine_s[hi, where, t].astype(F32) * weights[0][t : t + 1]
                for k in range(3):
                    block = block + got_s[hi, k, t].astype(F32) * weights[k + 1][t : t + 1]
                next_s[hi, t // 2, t % 2] = block.astype(BF16)
            for group in range(4):
                next_l[hi, group] = jnp.concatenate([joined[group * 2 : group * 2 + 2], zeros6], axis=0)

    def send_second(hi):
        sent = []
        for k in range(3):
            to_x, to_y = (x + k + 1) % 4, (y + k + 1) % 4
            for m, (src, dst, peer) in enumerate((
                (sa2.at[hi, to_y], ra2.at[hi, k], y_peers[k]),
                (sb2.at[hi, to_x], rb2.at[hi, k], x_peers[k]),
                (la2.at[hi, to_y], rla2.at[hi, k], y_peers[k]),
                (lb2.at[hi, to_x], rlb2.at[hi, k], x_peers[k]),
            )):
                sent.append(remote(src, dst, r2_ssem.at[hi, m, k], r2_rsem.at[hi, m, k], peer))
        for copy in sent:
            copy.start()
        return sent

    left64 = lane < 64

    def merge_second(hi):
        sides = []
        for mine_s, mine_l, got_s, got_l, where in ((sa2, la2, ra2, rla2, y), (sb2, lb2, rb2, rlb2, x)):
            weights, joined = shares([mine_l[hi, where]] + [got_l[hi, k] for k in range(3)])
            blocks = []
            for zp in range(2):
                block = mine_s[hi, where, zp].astype(F32) * weights[0][zp : zp + 1]
                for k in range(3):
                    block = block + got_s[hi, k, zp].astype(F32) * weights[k + 1][zp : zp + 1]
                blocks.append(block)
            sides.append((blocks, joined))
        for zp in range(2):
            a, b = sides[0][0][zp], sides[1][0][zp]
            s3[hi * 4 + zp * 2] = jnp.where(left64, a, pltpu.roll(b, 64, 1)).astype(BF16)
            s3[hi * 4 + zp * 2 + 1] = jnp.where(left64, pltpu.roll(a, 64, 1), b).astype(BF16)
            a, b = sides[0][1], sides[1][1]
            l3[hi * 4 + zp * 2] = jnp.where(lane8 < 64, a, pltpu.roll(b, 64, 1))[zp : zp + 1]
            l3[hi * 4 + zp * 2 + 1] = jnp.where(lane8 < 64, pltpu.roll(a, 64, 1), b)[zp : zp + 1]

    for copy in g3[0]:
        copy.wait()
    prompt_part(0)
    r1_low = send_first(0)
    for copy in g3[1]:
        copy.wait()
    prompt_part(1)
    r1_high = send_first(1)
    for copy in ret:
        copy.wait()
    back = [ret_rcv[bit, s].astype(F32) for s in range(4)]
    for j in range(4):
        for s in range(4):
            out[j, s] = jnp.where(my_slot == j, back[s], ret_loc[j, s].astype(F32)).astype(BF16)
    for copy in r1_low:
        copy.wait()
    merge_first(0)
    r2_low = send_second(0)
    for copy in r1_high:
        copy.wait()
    merge_first(1)
    r2_high = send_second(1)
    for copy in r2_low:
        copy.wait()
    merge_second(0)
    for copy in r2_high:
        copy.wait()
    merge_second(1)

    rz = []
    for k in range(7):
        to = (z + k + 1) % 8
        rz.append(remote(s3.at[to], r3.at[k], rz_ssem.at[0, k], rz_rsem.at[0, k], z_peers[k]))
        rz.append(remote(l3.at[to], rl3.at[k], rz_ssem.at[1, k], rz_rsem.at[1, k], z_peers[k]))
    for copy in rz:
        copy.start()
    for copy in rz:
        copy.wait()
    weights, _ = shares([new_lse, l3[z]] + [rl3[k] for k in range(7)])
    block = new_acc * weights[0] + s3[z].astype(F32) * weights[1]
    for k in range(7):
        block = block + r3[k].astype(F32) * weights[k + 2]
    flat = jnp.concatenate([block, block], axis=0).T
    here = jnp.where(left64, flat[:64], flat[64:])
    for s in range(4):
        out[4, s] = jnp.concatenate([here[s * 8 : s * 8 + 8], here[32 + s * 8 : 40 + s * 8]], axis=0).astype(BF16)


def per_device(
    pool_kv, block_table, context_len, partner, mig_slot, prompt_kv, prompt_dest, queries, step_kv
):
    smem = pl.BlockSpec(memory_space=pltpu.SMEM)
    vmem = pl.BlockSpec(memory_space=pltpu.VMEM)
    hbm = pl.BlockSpec(memory_space=pltpu.HBM)
    sem = lambda *shape: pltpu.SemaphoreType.DMA(shape)
    V = pltpu.VMEM
    return pl.pallas_call(
        body,
        out_shape=jax.ShapeDtypeStruct((5, 4, 16, HD), BF16),
        in_specs=[smem] * 5 + [vmem] * 4 + [hbm] * 2,
        out_specs=vmem,
        scratch_shapes=[
            V((48, 2, 2, 64, HD), BF16),
            V((2, 2, 12, 2, 2, 64, HD), BF16),
            V((12, 8, HD), F32),
            V((8, HD), jnp.int32),
            pltpu.SMEM((8, HD), jnp.int32),
            V((4, 80, HD), BF16),
            V((80, HD), BF16),
            V((3, 80, HD), BF16),
            V((4, 4, 16, HD), BF16),
            V((4, 16, HD), BF16),
            V((3, 4, 16, HD), BF16),
            V((8, 32, HD), BF16),
            V((8, 32, HD), BF16),
            V((4, 4, 4, 32, HD), BF16),
            V((4, 4, 4, 32, HD), BF16),
            V((4, 4, 4, 32, HD), BF16),
            V((4, 4, 4, 32, HD), BF16),
            V((25, HD, HD), F32),
            V((25, 1, HD), F32),
            V((25, HD, HD), F32),
            V((25, 1, HD), F32),
            V((2, 4, 8, 64, HD), BF16),
            V((2, 4, 8, 64, HD), BF16),
            V((2, 4, 8, HD), F32),
            V((2, 4, 8, HD), F32),
            V((2, 3, 8, 64, HD), BF16),
            V((2, 3, 8, 64, HD), BF16),
            V((2, 3, 8, HD), F32),
            V((2, 3, 8, HD), F32),
            V((2, 4, 2, 64, HD), BF16),
            V((2, 4, 2, 64, HD), BF16),
            V((2, 4, 8, HD), F32),
            V((2, 4, 8, HD), F32),
            V((2, 3, 2, 64, HD), BF16),
            V((2, 3, 2, 64, HD), BF16),
            V((2, 3, 8, HD), F32),
            V((2, 3, 8, HD), F32),
            V((8, 64, HD), BF16),
            V((8, 1, HD), F32),
            V((7, 64, HD), BF16),
            V((7, 1, HD), F32),
            sem(4), sem(2), sem(2), sem(3), sem(3), sem(3), sem(3),
            sem(2, 7), sem(2, 7), sem(2, 2, 3), sem(2, 2, 3), sem(2, 2, 3), sem(2, 2, 3),
            sem(2, 4, 3), sem(2, 4, 3), sem(2, 4, 3), sem(2, 4, 3), sem(2, 7), sem(2, 7),
        ],
        compiler_params=pltpu.CompilerParams(
            collective_id=0, has_side_effects=True, vmem_limit_bytes=60 * 1024 * 1024
        ),
    )(
        prompt_dest.reshape(-1), context_len.T, partner, mig_slot, block_table,
        prompt_dest.reshape(24, HD), jnp.asarray(rope_row()), queries, step_kv.reshape(5, 16, HD),
        pool_kv, prompt_kv,
    )


def solution(mesh):
    placed = (
        P("inst", None, "tp", None, None),
        P("inst", None),
        P(),
        P(),
        P(),
        P(("inst", "tp"), None, None, None, None),
        P(),
        P("inst", None, "tp", None),
        P("inst", None, None, "tp", None),
    )
    return jax.shard_map(
        per_device,
        mesh=mesh,
        in_specs=placed,
        out_specs=P("inst", None, "tp", None),
        check_vma=False,
    )
```

time: 91.2 us -> 65.1 us (0.71)
  local copies, waits for them, and re-layouts: 9.24 us -> 1.53 us
  Pallas kernels: 70.3 us -> 63.3 us
  other arithmetic: 5.95 us -> 0 us
  between operations: 4.99 us -> 0.01 us
    pallas_call x1, Pallas kernels: 70.3 us -> 63.3 us  [per_device(): pl.pallas_call(body, out_shape=jax.ShapeDtypeStruct((5, 4, 16, HD), BF16)...]
    dynamic_slice x5 -> x0, local copies, waits for them, and re-layouts: 5.53 us -> none  [the longest x2 2.67 us: per_device(): mate_len = context_len[mate, mig_slot[mate]]]
    convert_element_type x3 -> x0, other arithmetic: 1.71 us -> none  [the longest x1 0.9 us: per_device(): qrot = rotate(queries.astype(F32), cosine, sine).astype(BF16)]
    reduce_sum x1 -> x0, other arithmetic: 1.36 us -> none  [per_device(): new_len = jnp.sum((dests == inst).astype(jnp.int32)) * 64]
    select_n x4 -> x0, other arithmetic: 1.29 us -> none  [the longest x1 1.25 us: per_device(): jnp.where(jnp.arange(4, dtype=jnp.int32) == my_slot, mate_len, own_len)]
    unnamed x3 -> x1, local copies, waits for them, and re-layouts: 2.53 us -> 1.53 us
where the time goes in v2:
time: 65.1 us; the launch traced here: 64.8 us
  Pallas kernels  63.3 us (97%)
  local copies, waits for them, and re-layouts  1.53 us (2%)
    pallas_call x1, Pallas kernels, per_device(): pl.pallas_call(body, out_shape=jax.ShapeDtypeStruct((5, 4, 16, HD), BF16)...  63.3 us
    unnamed x1, local copies, waits for them, and re-layouts  1.53 us

profile of v2, /device:TPU:2, one launch (start us, length us, event | category | flops | bytes accessed | tf_op | source)
XLA Modules:
  0.0 64.8 jit_solution(15670317801671186646)
XLA Ops:
  0.0 63.3 %shard_map.100 = bf16[5,4,16,128]{3,2,1,0:T(8,128)(2,1)} custom-call(s32[3072]{0:T(1024)} %bitcast.4, s32[4,64]{1,0:T(4,128)} %bitcast.7, s32[64]{0:T(128)} %partner.1, s32[64]{0:T(128)} %mig_slot.1, s32[4,24]{1,0:T(4,128)} %table.1, s32[24,128]{1,0:T(8,128)} %bitcast.5, f32[1,128]{1,0:T(1,128)} %constant.2.clone.freqs, bf16[5,4,16,128]{3,2,1,0:T(8,128)(2,1)} %queries.1, ...), custom_call_target="tpu_custom_call" | custom-call | tf_op jit(solution)/shard_map/pallas_call | solution.py:502
  63.3 1.5 %copy.12 = bf16[5,4,16,128]{3,2,1,0:T(8,128)(2,1)} copy(bf16[5,4,16,128]{3,2,1,0:T(8,128)(2,1)} %shard_map.100) | data formatting | bytes 163840

commit v3 on v2

--- a/solution.py
+++ b/solution.py
@@ -44,8 +44,8 @@
     return first, second
 
 
-def dot_nt(a, b):
-    return lax.dot_general(a, b, (((1,), (1,)), ((), ())), preferred_element_type=F32)
+def dot_nn(a, b):
+    return lax.dot_general(a, b, (((1,), (0,)), ((), ())), preferred_element_type=F32)
 
 
 def dot_tn(a, b):
@@ -68,13 +68,15 @@
 
 
 def body(
-    dests, lengths, partner, mig_slot, table, dest_grid, freqs, queries, step_kv, pool_hbm, prompt_hbm, out,
+    dests_in, lengths_in, partner_in, mig_slot_in, table_in, grid_in, freqs_in, queries_in, kv_in,
+    pool_hbm, prompt_hbm, out,
+    dests, lengths, partner, mig_slot, table, dest_grid, freqs, queries, step_kv,
     pool, pages, ab, index_v, index, mig_mine, mig_send, mig_rcv, ret_loc, ret_send, ret_rcv,
-    zqa, zqb, qa_low, qa_high, qb_low, qb_high, acc, lse, acc2, lse2,
+    zq, qa_low, qa_high, qb_low, qb_high, acc, lse, acc2, lse2,
     sa, sb, la, lb, ra, rb, rla, rlb,
     sa2, sb2, la2, lb2, ra2, rb2, rla2, rlb2,
     s3, l3, r3, rl3,
-    local_sem, core_ssem, core_rsem, mig_ssem, mig_rsem, ret_ssem, ret_rsem,
+    in_sem, local_sem, core_ssem, core_rsem, mig_ssem, mig_rsem, ret_ssem, ret_rsem,
     gz_ssem, gz_rsem, g2_ssem, g2_rsem, g3_ssem, g3_rsem,
     r1_ssem, r1_rsem, r2_ssem, r2_rsem, rz_ssem, rz_rsem,
 ):
@@ -108,6 +110,15 @@
             device_id=peer, device_id_type=MESH,
         )
 
+    inputs = [
+        pltpu.make_async_copy(src, dst, in_sem.at[n])
+        for n, (src, dst) in enumerate((
+            (grid_in, dest_grid), (freqs_in, freqs), (queries_in, queries), (mig_slot_in, mig_slot),
+            (partner_in, partner), (lengths_in, lengths), (dests_in, dests), (table_in, table), (kv_in, step_kv),
+        ))
+    ]
+    for copy in inputs:
+        copy.start()
     pool_copy = pltpu.make_async_copy(pool_hbm, pool, local_sem.at[0])
     pool_copy.start()
     own_copies = [
@@ -119,13 +130,10 @@
     for copy in own_copies:
         copy.start()
 
-    my_slot = mig_slot[inst]
-    mate = partner[inst]
-    mate_len = lengths[mig_slot[mate], mate]
-    own_len = [lengths[j, inst] for j in range(4)]
-    bit = jnp.where(mate // 4 != inst // 4, 2, jnp.where(mate // 2 != inst // 2, 1, 0))
     first_row = inst * 48 + z_hi * 24
 
+    for copy in inputs[:3]:
+        copy.wait()
     freq = freqs[...]
     lane8 = iota((8, HD), 1)
     line8 = iota((8, HD), 0)
@@ -152,31 +160,37 @@
             both = queries[slot, s].astype(F32)
             for h in range(2):
                 tiles[h][s] = turn(both[h * 8 : h * 8 + 8], cosine[s : s + 1], sine[s : s + 1])
-        return [jnp.concatenate(part, axis=0).astype(BF16) for part in tiles]
+        return [jnp.concatenate(part, axis=0) for part in tiles]
 
     named_here = jnp.where(dest_grid[...] == inst, 1.0, 0.0)
     new_len = jnp.sum(jnp.sum(named_here, axis=0, keepdims=True), axis=1, keepdims=True) * 64.0
     mine = turned_query(4, *tables(new_len))
-    zqa[z] = mine[0]
-    zqb[z] = mine[1]
+    twice = jnp.concatenate(mine + mine, axis=0).T
+    zq[z] = jnp.where(iota((64, HD), 1) < 64, twice[:64], twice[64:]).astype(BF16)
+    twice = twice.astype(BF16)
     qa, qb = (qa_low, qa_high), (qb_low, qb_high)
 
     pl.semaphore_wait(barrier, len(everyone))
 
     gz = []
     for k in range(7):
-        here = zqa.at[z]
-        gz.append(remote(here, here, gz_ssem.at[0, k], gz_rsem.at[0, k], z_peers[k]))
-        here = zqb.at[z]
-        gz.append(remote(here, here, gz_ssem.at[1, k], gz_rsem.at[1, k], z_peers[k]))
+        gz.append(remote(zq.at[z], zq.at[z], gz_ssem.at[k], gz_rsem.at[k], z_peers[k]))
     for copy in gz:
         copy.start()
+    for copy in inputs[3:]:
+        copy.wait()
+
+    my_slot = mig_slot[inst]
+    mate = partner[inst]
+    mate_len = lengths[mig_slot[mate], mate]
+    own_len = [lengths[j, inst] for j in range(4)]
+    bit = jnp.where(mate // 4 != inst // 4, 2, jnp.where(mate // 2 != inst // 2, 1, 0))
 
     for j in range(4):
         length = jnp.where(my_slot == j, mate_len, own_len[j]).astype(F32)
         part = turned_query(j, *tables(length))
-        mig_mine[j, pl.ds(0, 32)] = part[0]
-        mig_mine[j, pl.ds(32, 32)] = part[1]
+        mig_mine[j, pl.ds(0, 32)] = part[0].astype(BF16)
+        mig_mine[j, pl.ds(32, 32)] = part[1].astype(BF16)
         mig_mine[j, pl.ds(64, 16)] = turn(step_kv[j].astype(F32), *key_tables(length)).astype(BF16)
     mig_send[...] = mig_mine[my_slot]
     mig = [remote(mig_send, mig_rcv.at[k], mig_ssem.at[k], mig_rsem.at[k], mig_peers[k]) for k in range(3)]
@@ -202,11 +216,10 @@
     index_copy = pltpu.make_async_copy(index_v, index, local_sem.at[3])
     index_copy.start()
 
-    twice = jnp.concatenate(mine + mine, axis=0)
     own_kv = turn(step_kv[4].astype(F32), *key_tables(new_len)).astype(BF16)
     lane16 = iota((16, HD), 1)
     ok = is_key & (line16 % 2 == (lane16 % 64) // 32) & (line16 // 4 <= (lane16 % 32) // 8)
-    score = jnp.where(ok, dot_nt(own_kv, twice) * SCALE, NEG)
+    score = jnp.where(ok, dot_nn(own_kv, twice) * SCALE, NEG)
     top = jnp.max(score, axis=0, keepdims=True)
     weight = jnp.where(ok, jnp.exp(score - top), 0.0).astype(BF16).astype(F32)
     total = jnp.sum(weight, axis=0, keepdims=True)
@@ -239,26 +252,28 @@
     lax.fori_loop(0, 24, count_step, 0)
 
     for copy in gz:
-        copy.wait()
-    g2 = []
+        copy.wait_recv()
+    g2 = [[], []]
     for hi in range(2):
+        part = zq.at[pl.ds(hi * 4, 4), pl.ds(0, 32)]
+        other = zq.at[pl.ds(hi * 4, 4), pl.ds(32, 32)]
         for k in range(3):
-            here = zqa.at[pl.ds(hi * 4, 4)]
-            g2.append(remote(here, qa[hi].at[x, y], g2_ssem.at[hi, 0, k], g2_rsem.at[hi, 0, k], y_peers[k]))
-            here = zqb.at[pl.ds(hi * 4, 4)]
-            g2.append(remote(here, qb[hi].at[y, x], g2_ssem.at[hi, 1, k], g2_rsem.at[hi, 1, k], x_peers[k]))
-    for copy in g2:
-        copy.start()
+            g2[hi].append(remote(part, qa[hi].at[x, y], g2_ssem.at[hi, 0, k], g2_rsem.at[hi, 0, k], y_peers[k]))
+            g2[hi].append(remote(other, qb[hi].at[y, x], g2_ssem.at[hi, 1, k], g2_rsem.at[hi, 1, k], x_peers[k]))
+        for copy in g2[hi]:
+            copy.start()
     for hi in range(2):
-        qa[hi][x, y] = zqa[pl.ds(hi * 4, 4)]
-        qb[hi][y, x] = zqb[pl.ds(hi * 4, 4)]
+        qa[hi][x, y] = zq[pl.ds(hi * 4, 4), pl.ds(0, 32)]
+        qb[hi][y, x] = zq[pl.ds(hi * 4, 4), pl.ds(32, 32)]
     for copy in mig:
-        copy.wait()
+        copy.wait_recv()
 
     came = mig_rcv[bit].astype(F32)
-    blocks = [jnp.where(my_slot == j, came, mig_mine[j].astype(F32)).astype(BF16) for j in range(4)]
-    fresh_kv = jnp.concatenate([block[64:80] for block in blocks], axis=0)
-    q_res = [jnp.concatenate([block[h * 32 : h * 32 + 32] for block in blocks], axis=0) for h in range(2)]
+    blocks = [jnp.where(my_slot == j, came, mig_mine[j].astype(F32)) for j in range(4)]
+    fresh_kv = jnp.concatenate([block[64:80] for block in blocks], axis=0).astype(BF16)
+    q_res = [
+        jnp.concatenate([block[h * 32 : h * 32 + 32] for block in blocks], axis=0).T.astype(BF16) for h in range(2)
+    ]
     pool_copy.wait()
     below = (iota((64, HD), 0) < rem).astype(F32)
 
@@ -271,7 +286,7 @@
             best, total, summed = carry[3 * h : 3 * h + 3]
             keys = pool[pl.ds(i * 4, 4), 0, h].reshape(256, HD)
             values = pool[pl.ds(i * 4, 4), 1, h].reshape(256, HD)
-            score = jnp.where(real, dot_nt(keys, q_res[h]) * SCALE, NEG)
+            score = jnp.where(real, dot_nn(keys, q_res[h]) * SCALE, NEG)
             top = jnp.maximum(best, jnp.max(score, axis=0, keepdims=True))
             weight = (count * jnp.exp(score - top)).astype(BF16)
             shrink = jnp.exp(best - top)
@@ -282,10 +297,10 @@
 
     start = (jnp.full((1, HD), NEG, F32), jnp.zeros((1, HD), F32), jnp.zeros((HD, HD), F32)) * 2
     state = lax.fori_loop(0, 4, res_step, start)
-    for copy in g2:
-        copy.wait()
     g3 = [[], []]
     for hi in range(2):
+        for copy in g2[hi]:
+            copy.wait_recv()
         for k in range(3):
             here = qa[hi].at[x]
             g3[hi].append(remote(here, here, g3_ssem.at[hi, 0, k], g3_rsem.at[hi, 0, k], x_peers[k]))
@@ -302,7 +317,7 @@
     for h in range(2):
         best, total, summed = state[3 * h : 3 * h + 3]
         ok = ok_slot & (line % 2 == h)
-        score = jnp.where(ok, dot_nt(fresh_kv, q_res[h]) * SCALE, NEG)
+        score = jnp.where(ok, dot_nn(fresh_kv, q_res[h]) * SCALE, NEG)
         top = jnp.maximum(best, jnp.max(score, axis=0, keepdims=True))
         weight = jnp.where(ok, jnp.exp(score - top), 0.0).astype(BF16).astype(F32)
         shrink = jnp.exp(best - top)
@@ -318,8 +333,10 @@
     for copy in ret:
         copy.start()
 
-    for copy in own_copies + core_copies:
+    for copy in own_copies:
         copy.wait()
+    for copy in core_copies:
+        copy.wait_recv()
     index_copy.wait()
     acc[24] = jnp.zeros((HD, HD), F32)
     acc2[24] = jnp.zeros((HD, HD), F32)
@@ -328,15 +345,17 @@
     same_head = iota((HD, HD), 0) // 64 == (iota((HD, HD), 1) % 64) // 32
     left = iota((HD, HD), 1) < 64
     left1 = lane1 < 64
+    left64 = lane < 64
     zeros6 = jnp.zeros((6, HD), F32)
 
     def prompt_part(hi):
         def page(n, src, i):
             d = dests[first_row + n]
             zl, dy, dx = d // 16, (d // 4) % 4, d % 4
-            half = [qa[hi][dx, dy, zl], qb[hi][dy, dx, zl]]
-            asked = jnp.concatenate(half + half, axis=0)
-            score = jnp.where(same_head, dot_nt(pages[src, hi, i, 0].reshape(HD, HD), asked) * SCALE, NEG)
+            part = jnp.concatenate([qa[hi][dx, dy, zl], qb[hi][dy, dx, zl]], axis=0)
+            swap = jnp.concatenate([part[:, 64:], part[:, :64]], axis=1)
+            asked = jnp.concatenate([jnp.where(left64, part, swap), jnp.where(left64, swap, part)], axis=0)
+            score = jnp.where(same_head, dot_nn(pages[src, hi, i, 0].reshape(HD, HD), asked) * SCALE, NEG)
             top = jnp.max(score, axis=0, keepdims=True)
             weight = jnp.exp(score - top).astype(BF16)
             total = jnp.sum(weight.astype(F32), axis=0, keepdims=True)
@@ -421,8 +440,6 @@
         for copy in sent:
             copy.start()
         return sent
-
-    left64 = lane < 64
 
     def merge_second(hi):
         sides = []
@@ -444,32 +461,34 @@
             l3[hi * 4 + zp * 2 + 1] = jnp.where(lane8 < 64, pltpu.roll(a, 64, 1), b)[zp : zp + 1]
 
     for copy in g3[0]:
-        copy.wait()
+        copy.wait_recv()
     prompt_part(0)
     r1_low = send_first(0)
     for copy in g3[1]:
-        copy.wait()
+        copy.wait_recv()
     prompt_part(1)
     r1_high = send_first(1)
+    for copy in gz + g2[0] + g2[1] + g3[0] + g3[1] + mig + core_copies:
+        copy.wait_send()
     for copy in ret:
-        copy.wait()
+        copy.wait_recv()
     back = [ret_rcv[bit, s].astype(F32) for s in range(4)]
     for j in range(4):
         for s in range(4):
             out[j, s] = jnp.where(my_slot == j, back[s], ret_loc[j, s].astype(F32)).astype(BF16)
     for copy in r1_low:
-        copy.wait()
+        copy.wait_recv()
     merge_first(0)
     r2_low = send_second(0)
     for copy in r1_high:
-        copy.wait()
+        copy.wait_recv()
     merge_first(1)
     r2_high = send_second(1)
     for copy in r2_low:
-        copy.wait()
+        copy.wait_recv()
     merge_second(0)
     for copy in r2_high:
-        copy.wait()
+        copy.wait_recv()
     merge_second(1)
 
     rz = []
@@ -479,8 +498,10 @@
         rz.append(remote(l3.at[to], rl3.at[k], rz_ssem.at[1, k], rz_rsem.at[1, k], z_peers[k]))
     for copy in rz:
         copy.start()
+    for copy in r1_low + r1_high + r2_low + r2_high + ret:
+        copy.wait_send()
     for copy in rz:
-        copy.wait()
+        copy.wait_recv()
     weights, _ = shares([new_lse, l3[z]] + [rl3[k] for k in range(7)])
     block = new_acc * weights[0] + s3[z].astype(F32) * weights[1]
     for k in range(7):
@@ -489,12 +510,13 @@
     here = jnp.where(left64, flat[:64], flat[64:])
     for s in range(4):
         out[4, s] = jnp.concatenate([here[s * 8 : s * 8 + 8], here[32 + s * 8 : 40 + s * 8]], axis=0).astype(BF16)
+    for copy in rz:
+        copy.wait_send()
 
 
 def per_device(
     pool_kv, block_table, context_len, partner, mig_slot, prompt_kv, prompt_dest, queries, step_kv
 ):
-    smem = pl.BlockSpec(memory_space=pltpu.SMEM)
     vmem = pl.BlockSpec(memory_space=pltpu.VMEM)
     hbm = pl.BlockSpec(memory_space=pltpu.HBM)
     sem = lambda *shape: pltpu.SemaphoreType.DMA(shape)
@@ -502,9 +524,18 @@
     return pl.pallas_call(
         body,
         out_shape=jax.ShapeDtypeStruct((5, 4, 16, HD), BF16),
-        in_specs=[smem] * 5 + [vmem] * 4 + [hbm] * 2,
+        in_specs=[hbm] * 11,
         out_specs=vmem,
         scratch_shapes=[
+            pltpu.SMEM((3072,), jnp.int32),
+            pltpu.SMEM((4, 64), jnp.int32),
+            pltpu.SMEM((64,), jnp.int32),
+            pltpu.SMEM((64,), jnp.int32),
+            pltpu.SMEM((4, 24), jnp.int32),
+            V((24, HD), jnp.int32),
+            V((1, HD), F32),
+            V((5, 4, 16, HD), BF16),
+            V((5, 16, HD), BF16),
             V((48, 2, 2, 64, HD), BF16),
             V((2, 2, 12, 2, 2, 64, HD), BF16),
             V((12, 8, HD), F32),
@@ -516,8 +547,7 @@
             V((4, 4, 16, HD), BF16),
             V((4, 16, HD), BF16),
             V((3, 4, 16, HD), BF16),
-            V((8, 32, HD), BF16),
-            V((8, 32, HD), BF16),
+            V((8, 64, HD), BF16),
             V((4, 4, 4, 32, HD), BF16),
             V((4, 4, 4, 32, HD), BF16),
             V((4, 4, 4, 32, HD), BF16),
@@ -546,8 +576,8 @@
             V((8, 1, HD), F32),
             V((7, 64, HD), BF16),
             V((7, 1, HD), F32),
-            sem(4), sem(2), sem(2), sem(3), sem(3), sem(3), sem(3),
-            sem(2, 7), sem(2, 7), sem(2, 2, 3), sem(2, 2, 3), sem(2, 2, 3), sem(2, 2, 3),
+            sem(9), sem(4), sem(2), sem(2), sem(3), sem(3), sem(3), sem(3),
+            sem(7), sem(7), sem(2, 2, 3), sem(2, 2, 3), sem(2, 2, 3), sem(2, 2, 3),
             sem(2, 4, 3), sem(2, 4, 3), sem(2, 4, 3), sem(2, 4, 3), sem(2, 7), sem(2, 7),
         ],
         compiler_params=pltpu.CompilerParams(

time: 65.1 us -> 59.2 us (0.909)
  Pallas kernels: 63.3 us -> 57.2 us
    pallas_call x1, Pallas kernels: 63.3 us -> 57.2 us  [per_device(): pl.pallas_call(body, out_shape=jax.ShapeDtypeStruct((5, 4, 16, HD), BF16)...]
where the time goes in v3:
time: 59.2 us; the launch traced here: 58.8 us
  Pallas kernels  57.2 us (97%)
  local copies, waits for them, and re-layouts  1.53 us (3%)
    pallas_call x1, Pallas kernels, per_device(): pl.pallas_call(body, out_shape=jax.ShapeDtypeStruct((5, 4, 16, HD), BF16)...  57.2 us
    unnamed x1, local copies, waits for them, and re-layouts  1.53 us

profile of v3, /device:TPU:2, one launch (start us, length us, event | category | flops | bytes accessed | tf_op | source)
XLA Modules:
  0.0 58.8 jit_solution(635725395668607843)
XLA Ops:
  0.0 57.2 %shard_map.100 = bf16[5,4,16,128]{3,2,1,0:T(8,128)(2,1)} custom-call(s32[3072]{0:T(1024)} %bitcast.4, s32[4,64]{1,0:T(4,128)} %bitcast.7, s32[64]{0:T(128)} %partner_in.1, s32[64]{0:T(128)} %mig_slot_in.1, s32[4,24]{1,0:T(4,128)} %table_in.1, s32[24,128]{1,0:T(8,128)} %bitcast.5, f32[1,128]{1,0:T(1,128)} %constant.2.clone.freqs_in, ...), custom_call_target="tpu_custom_call" | custom-call | tf_op jit(solution)/shard_map/pallas_call | solution.py:524
  57.2 1.5 %copy.12 = bf16[5,4,16,128]{3,2,1,0:T(8,128)(2,1)} copy(bf16[5,4,16,128]{3,2,1,0:T(8,128)(2,1)} %shard_map.100) | data formatting | bytes 163840

commit v4 on v3

--- a/solution.py
+++ b/solution.py
@@ -73,7 +73,7 @@
     dests, lengths, partner, mig_slot, table, dest_grid, freqs, queries, step_kv,
     pool, pages, ab, index_v, index, mig_mine, mig_send, mig_rcv, ret_loc, ret_send, ret_rcv,
     zq, qa_low, qa_high, qb_low, qb_high, acc, lse, acc2, lse2,
-    sa, sb, la, lb, ra, rb, rla, rlb,
+    sa, sb, la, lb, ra, rb, rla, rlb, ma, mb, mla, mlb,
     sa2, sb2, la2, lb2, ra2, rb2, rla2, rlb2,
     s3, l3, r3, rl3,
     in_sem, local_sem, core_ssem, core_rsem, mig_ssem, mig_rsem, ret_ssem, ret_rsem,
@@ -297,19 +297,35 @@
 
     start = (jnp.full((1, HD), NEG, F32), jnp.zeros((1, HD), F32), jnp.zeros((HD, HD), F32)) * 2
     state = lax.fori_loop(0, 4, res_step, start)
-    g3 = [[], []]
-    for hi in range(2):
-        for copy in g2[hi]:
-            copy.wait_recv()
-        for k in range(3):
-            here = qa[hi].at[x]
-            g3[hi].append(remote(here, here, g3_ssem.at[hi, 0, k], g3_rsem.at[hi, 0, k], x_peers[k]))
-            here = qb[hi].at[y]
-            g3[hi].append(remote(here, here, g3_ssem.at[hi, 1, k], g3_rsem.at[hi, 1, k], y_peers[k]))
-        for copy in g3[hi]:
-            copy.start()
-
-    state = lax.fori_loop(4, 12, res_step, state)
+    right = ((x + 1) % 4, (y + 1) % 4)
+    left_by = ((x + 3) % 4, (y + 3) % 4)
+    right_peer, left_peer = (x_peers[0], y_peers[0]), (x_peers[2], y_peers[2])
+    place = (x, y)
+
+    def ring(hi, side, kind, row, peer):
+        part = (qa, qb)[side][hi].at[row]
+        return remote(part, part, g3_ssem.at[hi, side, kind], g3_rsem.at[hi, side, kind], peer)
+
+    g3 = [
+        [[ring(hi, side, 0, place[side], right_peer[side]) for side in range(2)],
+         [ring(hi, side, 1, place[side], left_peer[side]) for side in range(2)],
+         [ring(hi, side, 2, (left_by, right)[hi][side], (right_peer, left_peer)[hi][side]) for side in range(2)]]
+        for hi in range(2)
+    ]
+    for copy in g2[0]:
+        copy.wait_recv()
+    for copy in g3[0][0] + g3[0][1]:
+        copy.start()
+    for copy in g2[1]:
+        copy.wait_recv()
+    for copy in g3[1][1]:
+        copy.start()
+    state = lax.fori_loop(4, 8, res_step, state)
+    for copy in g3[0][0]:
+        copy.wait_recv()
+    for copy in g3[0][2] + g3[1][0]:
+        copy.start()
+    state = lax.fori_loop(8, 12, res_step, state)
     lane = iota((64, HD), 1)
     line = iota((64, HD), 0)
     ok_slot = (line // 16 == lane // 32) & ((line // 2) % 2 == 0) & ((line % 16) // 4 <= (lane % 32) // 8)
@@ -333,6 +349,11 @@
     for copy in ret:
         copy.start()
 
+    for copy in g3[1][1]:
+        copy.wait_recv()
+    for copy in g3[1][2]:
+        copy.start()
+
     for copy in own_copies:
         copy.wait()
     for copy in core_copies:
@@ -398,30 +419,52 @@
 
             lax.fori_loop(0, 4, place_step, 0)
 
+    sides = ((sa, la, ra, rla, ma, mla, x, sa2, la2), (sb, lb, rb, rlb, mb, mlb, y, sb2, lb2))
+
+    def first_copies(hi, side, kind, data, stat, peer):
+        _, _, got_s, got_l = sides[side][:4]
+        return [
+            remote(data, got_s.at[hi, kind], r1_ssem.at[hi, side, kind], r1_rsem.at[hi, side, kind], peer),
+            remote(stat, got_l.at[hi, kind], r1_ssem.at[hi, 2 + side, kind], r1_rsem.at[hi, 2 + side, kind], peer),
+        ]
+
     def send_first(hi):
-        sent = []
-        for k in range(3):
-            to_x, to_y = (x + k + 1) % 4, (y + k + 1) % 4
-            for m, (src, dst, peer) in enumerate((
-                (sa.at[hi, to_x], ra.at[hi, k], x_peers[k]),
-                (sb.at[hi, to_y], rb.at[hi, k], y_peers[k]),
-                (la.at[hi, to_x], rla.at[hi, k], x_peers[k]),
-                (lb.at[hi, to_y], rlb.at[hi, k], y_peers[k]),
-            )):
-                sent.append(remote(src, dst, r1_ssem.at[hi, m, k], r1_rsem.at[hi, m, k], peer))
-        for copy in sent:
+        sent = [[], []]
+        for side in range(2):
+            mine_s, mine_l = sides[side][:2]
+            ahead, behind = (right_peer, left_peer) if hi == 0 else (left_peer, right_peer)
+            back = ((left_by, right)[hi])[side]
+            far = (place[side] + 2) % 4
+            sent[0] += first_copies(hi, side, 0, mine_s.at[hi, far], mine_l.at[hi, far], ahead[side])
+            sent[1] += first_copies(hi, side, 1, mine_s.at[hi, back], mine_l.at[hi, back], behind[side])
+        for copy in sent[0] + sent[1]:
             copy.start()
         return sent
 
+    def pass_on(hi):
+        sent = []
+        for side in range(2):
+            mine_s, mine_l, got_s, got_l, mid_s, mid_l = sides[side][:6]
+            front = ((right, left_by)[hi])[side]
+            weights, joined = shares([mine_l[hi, front], got_l[hi, 0]])
+            for t in range(8):
+                block = mine_s[hi, front, t].astype(F32) * weights[0][t : t + 1]
+                block = block + got_s[hi, 0, t].astype(F32) * weights[1][t : t + 1]
+                mid_s[hi, t] = block.astype(BF16)
+            mid_l[hi] = joined
+            ahead = (right_peer, left_peer)[hi][side]
+            sent += first_copies(hi, side, 2, mid_s.at[hi], mid_l.at[hi], ahead)
+            for copy in sent[-2:]:
+                copy.start()
+        return sent
+
     def merge_first(hi):
-        for mine_s, mine_l, got_s, got_l, where, next_s, next_l in (
-            (sa, la, ra, rla, x, sa2, la2), (sb, lb, rb, rlb, y, sb2, lb2)
-        ):
-            weights, joined = shares([mine_l[hi, where]] + [got_l[hi, k] for k in range(3)])
+        for mine_s, mine_l, got_s, got_l, _, _, where, next_s, next_l in sides:
+            weights, joined = shares([mine_l[hi, where], got_l[hi, 1], got_l[hi, 2]])
             for t in range(8):
                 block = mine_s[hi, where, t].astype(F32) * weights[0][t : t + 1]
-                for k in range(3):
-                    block = block + got_s[hi, k, t].astype(F32) * weights[k + 1][t : t + 1]
+                for k in range(1, 3):
+                    block = block + got_s[hi, k, t].astype(F32) * weights[k][t : t + 1]
                 next_s[hi, t // 2, t % 2] = block.astype(BF16)
             for group in range(4):
                 next_l[hi, group] = jnp.concatenate([joined[group * 2 : group * 2 + 2], zeros6], axis=0)
@@ -442,7 +485,7 @@
         return sent
 
     def merge_second(hi):
-        sides = []
+        both = []
         for mine_s, mine_l, got_s, got_l, where in ((sa2, la2, ra2, rla2, y), (sb2, lb2, rb2, rlb2, x)):
             weights, joined = shares([mine_l[hi, where]] + [got_l[hi, k] for k in range(3)])
             blocks = []
@@ -451,24 +494,30 @@
                 for k in range(3):
                     block = block + got_s[hi, k, zp].astype(F32) * weights[k + 1][zp : zp + 1]
                 blocks.append(block)
-            sides.append((blocks, joined))
+            both.append((blocks, joined))
         for zp in range(2):
-            a, b = sides[0][0][zp], sides[1][0][zp]
+            a, b = both[0][0][zp], both[1][0][zp]
             s3[hi * 4 + zp * 2] = jnp.where(left64, a, pltpu.roll(b, 64, 1)).astype(BF16)
             s3[hi * 4 + zp * 2 + 1] = jnp.where(left64, pltpu.roll(a, 64, 1), b).astype(BF16)
-            a, b = sides[0][1], sides[1][1]
+            a, b = both[0][1], both[1][1]
             l3[hi * 4 + zp * 2] = jnp.where(lane8 < 64, a, pltpu.roll(b, 64, 1))[zp : zp + 1]
             l3[hi * 4 + zp * 2 + 1] = jnp.where(lane8 < 64, pltpu.roll(a, 64, 1), b)[zp : zp + 1]
 
-    for copy in g3[0]:
+    for copy in g3[0][1] + g3[0][2]:
         copy.wait_recv()
     prompt_part(0)
     r1_low = send_first(0)
-    for copy in g3[1]:
+    for copy in g3[1][0] + g3[1][2]:
         copy.wait_recv()
     prompt_part(1)
     r1_high = send_first(1)
-    for copy in gz + g2[0] + g2[1] + g3[0] + g3[1] + mig + core_copies:
+    for copy in r1_low[0]:
+        copy.wait_recv()
+    r1_low.append(pass_on(0))
+    for copy in r1_high[0]:
+        copy.wait_recv()
+    r1_high.append(pass_on(1))
+    for copy in gz + g2[0] + g2[1] + g3[0][0] + g3[0][1] + g3[0][2] + g3[1][0] + g3[1][1] + g3[1][2] + mig + core_copies:
         copy.wait_send()
     for copy in ret:
         copy.wait_recv()
@@ -476,11 +525,11 @@
     for j in range(4):
         for s in range(4):
             out[j, s] = jnp.where(my_slot == j, back[s], ret_loc[j, s].astype(F32)).astype(BF16)
-    for copy in r1_low:
+    for copy in r1_low[1] + r1_low[2]:
         copy.wait_recv()
     merge_first(0)
     r2_low = send_second(0)
-    for copy in r1_high:
+    for copy in r1_high[1] + r1_high[2]:
         copy.wait_recv()
     merge_first(1)
     r2_high = send_second(1)
@@ -498,7 +547,7 @@
         rz.append(remote(l3.at[to], rl3.at[k], rz_ssem.at[1, k], rz_rsem.at[1, k], z_peers[k]))
     for copy in rz:
         copy.start()
-    for copy in r1_low + r1_high + r2_low + r2_high + ret:
+    for copy in sum(r1_low + r1_high, []) + r2_low + r2_high + ret:
         copy.wait_send()
     for copy in rz:
         copy.wait_recv()
@@ -564,6 +613,10 @@
             V((2, 3, 8, 64, HD), BF16),
             V((2, 3, 8, HD), F32),
             V((2, 3, 8, HD), F32),
+            V((2, 8, 64, HD), BF16),
+            V((2, 8, 64, HD), BF16),
+            V((2, 8, HD), F32),
+            V((2, 8, HD), F32),
             V((2, 4, 2, 64, HD), BF16),
             V((2, 4, 2, 64, HD), BF16),
             V((2, 4, 8, HD), F32),

time: 59.2 us -> 59.5 us (level)
  Pallas kernels: 57.2 us -> 57.9 us
    pallas_call x1, Pallas kernels: 57.2 us -> 57.9 us  [per_device(): pl.pallas_call(body, out_shape=jax.ShapeDtypeStruct((5, 4, 16, HD), BF16)...]
where the time goes in v4:
time: 59.5 us; the launch traced here: 59.4 us
  Pallas kernels  57.9 us (97%)
  local copies, waits for them, and re-layouts  1.53 us (3%)
    pallas_call x1, Pallas kernels, per_device(): pl.pallas_call(body, out_shape=jax.ShapeDtypeStruct((5, 4, 16, HD), BF16)...  57.9 us
    unnamed x1, local copies, waits for them, and re-layouts  1.53 us

profile of v4, /device:TPU:2, one launch (start us, length us, event | category | flops | bytes accessed | tf_op | source)
XLA Modules:
  0.0 59.4 jit_solution(11768614614999478437)
XLA Ops:
  0.0 57.9 %shard_map.100 = bf16[5,4,16,128]{3,2,1,0:T(8,128)(2,1)} custom-call(s32[3072]{0:T(1024)} %bitcast.4, s32[4,64]{1,0:T(4,128)} %bitcast.7, s32[64]{0:T(128)} %partner_in.1, s32[64]{0:T(128)} %mig_slot_in.1, s32[4,24]{1,0:T(4,128)} %table_in.1, s32[24,128]{1,0:T(8,128)} %bitcast.5, f32[1,128]{1,0:T(1,128)} %constant.2.clone.freqs_in, ...), custom_call_target="tpu_custom_call" | custom-call | tf_op jit(solution)/shard_map/pallas_call | solution.py:573
  57.9 1.5 %copy.12 = bf16[5,4,16,128]{3,2,1,0:T(8,128)(2,1)} copy(bf16[5,4,16,128]{3,2,1,0:T(8,128)(2,1)} %shard_map.100) | data formatting | bytes 163840

commit v5 on v3

--- a/solution.py
+++ b/solution.py
@@ -227,30 +227,6 @@
     new_acc = jnp.where(iota((64, HD), 1) < 64, new_acc[:64], new_acc[64:])
     new_lse = top + jnp.log(total)
 
-    shape = (12, 8, HD)
-    row = iota(shape, 1)
-    page_id = iota(shape, 0) * 4 + row % 4
-    is_last = row // 4
-    lane1 = lane8[:1]
-
-    def by_slot(values):
-        return jnp.where(
-            lane1 < 64, jnp.where(lane1 < 32, values[0], values[1]), jnp.where(lane1 < 96, values[2], values[3])
-        )
-
-    context = by_slot(own_len)
-    full, rem = context // 64, context % 64
-    ab[...] = jnp.zeros(shape, F32)
-
-    def count_step(k, carry):
-        named = by_slot([table[j, k] for j in range(4)])[None]
-        kind = jnp.where(k < full, 0, jnp.where(k == full, 1, 2))[None]
-        hit = (page_id == named) & (is_last == kind)
-        ab[...] += jnp.where(hit, 1.0, 0.0)
-        return carry
-
-    lax.fori_loop(0, 24, count_step, 0)
-
     for copy in gz:
         copy.wait_recv()
     g2 = [[], []]
@@ -265,6 +241,30 @@
     for hi in range(2):
         qa[hi][x, y] = zq[pl.ds(hi * 4, 4), pl.ds(0, 32)]
         qb[hi][y, x] = zq[pl.ds(hi * 4, 4), pl.ds(32, 32)]
+    shape = (12, 8, HD)
+    row = iota(shape, 1)
+    page_id = iota(shape, 0) * 4 + row % 4
+    is_last = row // 4
+    lane1 = lane8[:1]
+
+    def by_slot(values):
+        return jnp.where(
+            lane1 < 64, jnp.where(lane1 < 32, values[0], values[1]), jnp.where(lane1 < 96, values[2], values[3])
+        )
+
+    context = by_slot(own_len)
+    full, rem = context // 64, context % 64
+    ab[...] = jnp.zeros(shape, F32)
+
+    def count_step(k, carry):
+        named = by_slot([table[j, k] for j in range(4)])[None]
+        kind = jnp.where(k < full, 0, jnp.where(k == full, 1, 2))[None]
+        hit = (page_id == named) & (is_last == kind)
+        ab[...] += jnp.where(hit, 1.0, 0.0)
+        return carry
+
+    lax.fori_loop(0, 24, count_step, 0)
+
     for copy in mig:
         copy.wait_recv()
 
@@ -278,14 +278,16 @@
     below = (iota((64, HD), 0) < rem).astype(F32)
 
     def res_step(i, carry):
-        named = ab[i]
-        count = (named[0:4][:, None, :] + named[4:8][:, None, :] * below[None]).reshape(256, HD)
+        named = [ab[i * 2 + n] for n in range(2)]
+        count = jnp.concatenate(
+            [(part[0:4][:, None, :] + part[4:8][:, None, :] * below[None]).reshape(256, HD) for part in named], axis=0
+        )
         real = count > 0.0
         after = []
         for h in range(2):
             best, total, summed = carry[3 * h : 3 * h + 3]
-            keys = pool[pl.ds(i * 4, 4), 0, h].reshape(256, HD)
-            values = pool[pl.ds(i * 4, 4), 1, h].reshape(256, HD)
+            keys = pool[pl.ds(i * 8, 8), 0, h].reshape(512, HD)
+            values = pool[pl.ds(i * 8, 8), 1, h].reshape(512, HD)
             score = jnp.where(real, dot_nn(keys, q_res[h]) * SCALE, NEG)
             top = jnp.maximum(best, jnp.max(score, axis=0, keepdims=True))
             weight = (count * jnp.exp(score - top)).astype(BF16)
@@ -296,20 +298,36 @@
         return tuple(after)
 
     start = (jnp.full((1, HD), NEG, F32), jnp.zeros((1, HD), F32), jnp.zeros((HD, HD), F32)) * 2
-    state = lax.fori_loop(0, 4, res_step, start)
-    g3 = [[], []]
-    for hi in range(2):
-        for copy in g2[hi]:
-            copy.wait_recv()
-        for k in range(3):
-            here = qa[hi].at[x]
-            g3[hi].append(remote(here, here, g3_ssem.at[hi, 0, k], g3_rsem.at[hi, 0, k], x_peers[k]))
-            here = qb[hi].at[y]
-            g3[hi].append(remote(here, here, g3_ssem.at[hi, 1, k], g3_rsem.at[hi, 1, k], y_peers[k]))
-        for copy in g3[hi]:
-            copy.start()
-
-    state = lax.fori_loop(4, 12, res_step, state)
+    state = lax.fori_loop(0, 2, res_step, start)
+    right = ((x + 1) % 4, (y + 1) % 4)
+    left_by = ((x + 3) % 4, (y + 3) % 4)
+    right_peer, left_peer = (x_peers[0], y_peers[0]), (x_peers[2], y_peers[2])
+    place = (x, y)
+
+    def ring(hi, side, kind, row, peer):
+        part = (qa, qb)[side][hi].at[row]
+        return remote(part, part, g3_ssem.at[hi, side, kind], g3_rsem.at[hi, side, kind], peer)
+
+    g3 = [
+        [[ring(hi, side, 0, place[side], right_peer[side]) for side in range(2)],
+         [ring(hi, side, 1, place[side], left_peer[side]) for side in range(2)],
+         [ring(hi, side, 2, (left_by, right)[hi][side], (right_peer, left_peer)[hi][side]) for side in range(2)]]
+        for hi in range(2)
+    ]
+    for copy in g2[0]:
+        copy.wait_recv()
+    for copy in g3[0][0] + g3[0][1]:
+        copy.start()
+    for copy in g2[1]:
+        copy.wait_recv()
+    for copy in g3[1][1]:
+        copy.start()
+    state = lax.fori_loop(2, 4, res_step, state)
+    for copy in g3[0][0]:
+        copy.wait_recv()
+    for copy in g3[0][2]:
+        copy.start()
+    state = lax.fori_loop(4, 6, res_step, state)
     lane = iota((64, HD), 1)
     line = iota((64, HD), 0)
     ok_slot = (line // 16 == lane // 32) & ((line // 2) % 2 == 0) & ((line % 16) // 4 <= (lane % 32) // 8)
@@ -333,6 +351,11 @@
     for copy in ret:
         copy.start()
 
+    for copy in g3[1][1]:
+        copy.wait_recv()
+    for copy in g3[1][2] + g3[1][0]:
+        copy.start()
+
     for copy in own_copies:
         copy.wait()
     for copy in core_copies:
@@ -442,7 +465,7 @@
         return sent
 
     def merge_second(hi):
-        sides = []
+        both = []
         for mine_s, mine_l, got_s, got_l, where in ((sa2, la2, ra2, rla2, y), (sb2, lb2, rb2, rlb2, x)):
             weights, joined = shares([mine_l[hi, where]] + [got_l[hi, k] for k in range(3)])
             blocks = []
@@ -451,24 +474,24 @@
                 for k in range(3):
                     block = block + got_s[hi, k, zp].astype(F32) * weights[k + 1][zp : zp + 1]
                 blocks.append(block)
-            sides.append((blocks, joined))
+            both.append((blocks, joined))
         for zp in range(2):
-            a, b = sides[0][0][zp], sides[1][0][zp]
+            a, b = both[0][0][zp], both[1][0][zp]
             s3[hi * 4 + zp * 2] = jnp.where(left64, a, pltpu.roll(b, 64, 1)).astype(BF16)
             s3[hi * 4 + zp * 2 + 1] = jnp.where(left64, pltpu.roll(a, 64, 1), b).astype(BF16)
-            a, b = sides[0][1], sides[1][1]
+            a, b = both[0][1], both[1][1]
             l3[hi * 4 + zp * 2] = jnp.where(lane8 < 64, a, pltpu.roll(b, 64, 1))[zp : zp + 1]
             l3[hi * 4 + zp * 2 + 1] = jnp.where(lane8 < 64, pltpu.roll(a, 64, 1), b)[zp : zp + 1]
 
-    for copy in g3[0]:
+    for copy in g3[0][1] + g3[0][2]:
         copy.wait_recv()
     prompt_part(0)
     r1_low = send_first(0)
-    for copy in g3[1]:
+    for copy in g3[1][0] + g3[1][2]:
         copy.wait_recv()
     prompt_part(1)
     r1_high = send_first(1)
-    for copy in gz + g2[0] + g2[1] + g3[0] + g3[1] + mig + core_copies:
+    for copy in gz + g2[0] + g2[1] + g3[0][0] + g3[0][1] + g3[0][2] + g3[1][0] + g3[1][1] + g3[1][2] + mig + core_copies:
         copy.wait_send()
     for copy in ret:
         copy.wait_recv()

time: 59.2 us -> 58.7 us (level)
  no operation moved by 1% of the time
where the time goes in v5:
time: 58.7 us; the launch traced here: 58.6 us
  Pallas kernels  57 us (97%)
  local copies, waits for them, and re-layouts  1.53 us (3%)
    pallas_call x1, Pallas kernels, per_device(): pl.pallas_call(body, out_shape=jax.ShapeDtypeStruct((5, 4, 16, HD), BF16)...  57 us
    unnamed x1, local copies, waits for them, and re-layouts  1.53 us

profile of v5, /device:TPU:2, one launch (start us, length us, event | category | flops | bytes accessed | tf_op | source)
XLA Modules:
  0.0 58.6 jit_solution(10420695973245613711)
XLA Ops:
  0.0 57.0 %shard_map.100 = bf16[5,4,16,128]{3,2,1,0:T(8,128)(2,1)} custom-call(s32[3072]{0:T(1024)} %bitcast.4, s32[4,64]{1,0:T(4,128)} %bitcast.7, s32[64]{0:T(128)} %partner_in.1, s32[64]{0:T(128)} %mig_slot_in.1, s32[4,24]{1,0:T(4,128)} %table_in.1, s32[24,128]{1,0:T(8,128)} %bitcast.5, f32[1,128]{1,0:T(1,128)} %constant.2.clone.freqs_in, ...), custom_call_target="tpu_custom_call" | custom-call | tf_op jit(solution)/shard_map/pallas_call | solution.py:547
  57.0 1.5 %copy.12 = bf16[5,4,16,128]{3,2,1,0:T(8,128)(2,1)} copy(bf16[5,4,16,128]{3,2,1,0:T(8,128)(2,1)} %shard_map.100) | data formatting | bytes 163840

commit v6 on v5

--- a/solution.py
+++ b/solution.py
@@ -173,7 +173,7 @@
     pl.semaphore_wait(barrier, len(everyone))
 
     gz = []
-    for k in range(7):
+    for k in (3, 2, 4, 1, 5, 0, 6):
         gz.append(remote(zq.at[z], zq.at[z], gz_ssem.at[k], gz_rsem.at[k], z_peers[k]))
     for copy in gz:
         copy.start()
@@ -423,7 +423,7 @@
 
     def send_first(hi):
         sent = []
-        for k in range(3):
+        for k in (1, 0, 2):
             to_x, to_y = (x + k + 1) % 4, (y + k + 1) % 4
             for m, (src, dst, peer) in enumerate((
                 (sa.at[hi, to_x], ra.at[hi, k], x_peers[k]),
@@ -451,7 +451,7 @@
 
     def send_second(hi):
         sent = []
-        for k in range(3):
+        for k in (1, 0, 2):
             to_x, to_y = (x + k + 1) % 4, (y + k + 1) % 4
             for m, (src, dst, peer) in enumerate((
                 (sa2.at[hi, to_y], ra2.at[hi, k], y_peers[k]),
@@ -515,7 +515,7 @@
     merge_second(1)
 
     rz = []
-    for k in range(7):
+    for k in (3, 2, 4, 1, 5, 0, 6):
         to = (z + k + 1) % 8
         rz.append(remote(s3.at[to], r3.at[k], rz_ssem.at[0, k], rz_rsem.at[0, k], z_peers[k]))
         rz.append(remote(l3.at[to], rl3.at[k], rz_ssem.at[1, k], rz_rsem.at[1, k], z_peers[k]))

time: 58.7 us -> 57.3 us (0.976)
  Pallas kernels: 57 us -> 55.3 us
    pallas_call x1, Pallas kernels: 57 us -> 55.3 us  [per_device(): pl.pallas_call(body, out_shape=jax.ShapeDtypeStruct((5, 4, 16, HD), BF16)...]
where the time goes in v6:
time: 57.3 us; the launch traced here: 56.8 us
  Pallas kernels  55.3 us (97%)
  local copies, waits for them, and re-layouts  1.53 us (3%)
    pallas_call x1, Pallas kernels, per_device(): pl.pallas_call(body, out_shape=jax.ShapeDtypeStruct((5, 4, 16, HD), BF16)...  55.3 us
    unnamed x1, local copies, waits for them, and re-layouts  1.53 us

profile of v6, /device:TPU:2, one launch (start us, length us, event | category | flops | bytes accessed | tf_op | source)
XLA Modules:
  0.0 56.8 jit_solution(3532216184841334066)
XLA Ops:
  0.0 55.3 %shard_map.100 = bf16[5,4,16,128]{3,2,1,0:T(8,128)(2,1)} custom-call(s32[3072]{0:T(1024)} %bitcast.4, s32[4,64]{1,0:T(4,128)} %bitcast.7, s32[64]{0:T(128)} %partner_in.1, s32[64]{0:T(128)} %mig_slot_in.1, s32[4,24]{1,0:T(4,128)} %table_in.1, s32[24,128]{1,0:T(8,128)} %bitcast.5, f32[1,128]{1,0:T(1,128)} %constant.2.clone.freqs_in, ...), custom_call_target="tpu_custom_call" | custom-call | tf_op jit(solution)/shard_map/pallas_call | solution.py:547
  55.3 1.5 %copy.12 = bf16[5,4,16,128]{3,2,1,0:T(8,128)(2,1)} copy(bf16[5,4,16,128]{3,2,1,0:T(8,128)(2,1)} %shard_map.100) | data formatting | bytes 163840
